TPU v7x, 512 devices: a whole 4x8x8 slice. The times are simulated.
512 devices in a mesh: gx: 16 (over y_hi, x, core), gy: 8 (over z), gz: 4 (over y_lo).
Axes of the slice: x: 4, y: 8 (y_hi: 2, y_lo: 4; y = y_hi * 4 + y_lo), z: 8, core: 2. Of those that a mesh axis runs over, the one named last changes fastest.
Arguments:
- block_input: bfloat16 [1024, 14848], P('gx', ('gy', 'gz')), may hold values from -6 to 6
- context: bfloat16 [1024, 7424], P('gx', ('gy', 'gz')), may hold values from -6 to 6
- query_grad: bfloat16 [1024, 7424], P(('gy', 'gz'), 'gx'), may hold values from -6 to 6
- output_grad: bfloat16 [1024, 14848], P(('gy', 'gz'), 'gx'), may hold values from -6 to 6
- query_weight: bfloat16 [14848, 7424], P(('gy', 'gz'), 'gx'), may hold values from -0.046875 to 0.046875
- query_moment: bfloat16 [14848, 7424], P(('gy', 'gz'), 'gx'), may hold values from -0.59765625 to 0.59765625
- output_weight: bfloat16 [7424, 14848], P(('gy', 'gz'), 'gx'), may hold values from -0.0625 to 0.0625
- output_moment: bfloat16 [7424, 14848], P(('gy', 'gz'), 'gx'), may hold values from -0.59765625 to 0.59765625
Outputs:
- input_grad: bfloat16 [1024, 14848], P('gx', ('gy', 'gz'))
- context_grad: bfloat16 [1024, 7424], P('gx', ('gy', 'gz'))
- query_step: bfloat16 [14848, 7424], P(('gy', 'gz'), 'gx')
- query_momentum: bfloat16 [14848, 7424], P(('gy', 'gz'), 'gx')
- output_step: bfloat16 [7424, 14848], P(('gy', 'gz'), 'gx')
- output_momentum: bfloat16 [7424, 14848], P(('gy', 'gz'), 'gx')
All inputs are finite; a program needn't handle non-finite values.
Results may differ from a plain program's by a relative error of at most 0.001.
Values may be sent and summed in bfloat16 or wider, within the bound.
No kernel may reach another device: no remote copies, remote signals or barrier semaphores. Data moves between devices by JAX's collectives and lax.ppermute only.
A program may use at most 64 MiB of HBM per device.

v0:
```python
import math

import jax
import jax.numpy as jnp
from jax import lax
from jax.sharding import PartitionSpec as P


def lion_step(gradient, moment):
    held = moment.astype(jnp.float32)
    blended = 0.9 * held + 0.1 * gradient
    direction = blended / jnp.sqrt(blended * blended + 0.01)
    updated = 0.99 * held + 0.01 * gradient
    return (direction.astype(jnp.bfloat16), updated.astype(jnp.bfloat16))


def times_transposed(left, right):
    return lax.dot_general(
        left, right, (((1,), (1,)), ((), ())), preferred_element_type=jnp.float32
    )


def rows_product(left, right):
    return lax.dot_general(
        left, right, (((0,), (0,)), ((), ())), preferred_element_type=jnp.float32
    )


def on_device(
    block_input,
    context,
    query_grad,
    output_grad,
    query_weight,
    query_moment,
    output_weight,
    output_moment,
):
    query_all, output_all = (
        lax.all_gather(query_grad, ("gy", "gz"), axis=0, tiled=True),
        lax.all_gather(output_grad, ("gy", "gz"), axis=0, tiled=True),
    )
    query_term = times_transposed(query_all, query_weight)
    output_term = times_transposed(output_all, output_weight)
    input_sum, context_sum = (
        lax.psum_scatter(query_term, "gx", scatter_dimension=0, tiled=True),
        lax.psum_scatter(output_term, "gx", scatter_dimension=0, tiled=True),
    )
    input_grad = input_sum.astype(jnp.bfloat16)
    context_grad = context_sum.astype(jnp.bfloat16)
    query_sum = rows_product(lax.all_gather(block_input, "gx", axis=0, tiled=True), query_all)
    output_sum = rows_product(lax.all_gather(context, "gx", axis=0, tiled=True), output_all)
    norm_factor = 1.0 / math.sqrt(float(query_all.shape[0]))
    query_step, query_momentum = lion_step(query_sum * norm_factor, query_moment)
    output_step, output_momentum = lion_step(output_sum * norm_factor, output_moment)
    return (input_grad, context_grad, query_step, query_momentum, output_step, output_momentum)


def solution(mesh):
    in_specs = (
        P("gx", ("gy", "gz")),
        P("gx", ("gy", "gz")),
        P(("gy", "gz"), "gx"),
        P(("gy", "gz"), "gx"),
        P(("gy", "gz"), "gx"),
        P(("gy", "gz"), "gx"),
        P(("gy", "gz"), "gx"),
        P(("gy", "gz"), "gx"),
    )
    out_specs = (
        P("gx", ("gy", "gz")),
        P("gx", ("gy", "gz")),
        P(("gy", "gz"), "gx"),
        P(("gy", "gz"), "gx"),
        P(("gy", "gz"), "gx"),
        P(("gy", "gz"), "gx"),
    )
    return jax.shard_map(
        on_device, mesh=mesh, in_specs=in_specs, out_specs=out_specs, check_vma=False
    )
```

profile of v0, /device:TPU:2, one launch (start us, length us, event | category | flops | bytes accessed | tf_op | source)
XLA Modules:
  0.0 297.4 jit_solution(1245644805859589875)
XLA Ops:
  8.0 0.0 copy-start
  8.0 0.0 all-gather.2.cloned.1.call-start
  8.1 0.7 all-gather.2.cloned.1.call-update
  8.7 0.0 reduce-scatter.3.cloned.1.call-start
  8.8 96.9 %all_gather.12 = bf16[1024,464]{1,0:T(8,128)(2,1)S(1)} all-gather(bf16[32,464]{1,0:T(8,128)(2,1)} %param.10), channel_id=1, replica_groups=mesh['gx'=16,'gy'=8,'gz'=4] {'gy','gz'}, dimensions={0}, use_global_device_ids=true | all-gather | bytes 979968 | tf_op jit(solution)/shard_map/all_gather | solution.py:40
  105.7 0.0 copy-done
  105.7 2.1 fusion.6
  107.7 0.0 reduce-scatter.3.cloned.1.call-update
  107.8 0.0 copy-start.3
  107.8 0.0 copy-start.2
  107.8 0.0 reduce-scatter.5.cloned.1.call-start
  107.8 72.9 %all-gather.2.cloned.1.call-done = bf16[1024,928]{1,0:T(8,128)(2,1)} async-done(((bf16[32,928]{1,0:T(8,128)(2,1)}), bf16[1024,928]{1,0:T(8,128)(2,1)}) %all-gather.2.cloned.1.call-update) | async-done | bytes 1900560 | tf_op jit(solution)/shard_map/all_gather | solution.py:41
  180.8 0.0 copy-done.1
  180.8 3.3 %fusion.7 = f32[1024,232]{1,0:T(8,128)} fusion(bf16[1024,928]{1,0:T(8,128)(2,1)} %all-gather.2.cloned.1.call-done, bf16[232,928]{1,0:T(8,128)(2,1)S(1)} %copy-done.1), kind=kOutput, calls=%fused_computation.13 | convolution fusion | flops 440926208 | bytes 3281408 | tf_op jit(solution)/shard_map/dot_general | solution.py:18
  184.1 0.0 reduce-scatter.5.cloned.1.call-update
  184.1 0.0 copy-done.3
  184.1 25.7 %all_gather.15 = bf16[1024,232]{1,0:T(8,128)(2,1)S(1)} all-gather(bf16[64,232]{1,0:T(8,128)(2,1)S(1)} %copy-done.3), channel_id=1, replica_groups=mesh['gx'=16,'gy'=8,'gz'=4] {'gx'}, dimensions={0}, use_global_device_ids=true | all-gather | bytes 504832 | tf_op jit(solution)/shard_map/all_gather | solution.py:52
  209.8 0.0 copy-done.2
  209.8 36.5 %all_gather.14 = bf16[1024,464]{1,0:T(8,128)(2,1)S(1)} all-gather(bf16[64,464]{1,0:T(8,128)(2,1)S(1)} %copy-done.2), channel_id=1, replica_groups=mesh['gx'=16,'gy'=8,'gz'=4] {'gx'}, dimensions={0}, use_global_device_ids=true | all-gather | bytes 1009664 | tf_op jit(solution)/shard_map/all_gather | solution.py:51
  246.4 1.8 fusion.2
  248.2 1.5 convert_element_type.24
  249.7 3.4 %fusion.5 = (bf16[232,928]{1,0:T(8,128)(2,1)}, bf16[232,928]{1,0:T(8,128)(2,1)}) fusion(bf16[232,928]{1,0:T(8,128)(2,1)S(1)} %copy-done.5, bf16[1024,232]{1,0:T(8,128)(2,1)S(1)} %all_gather.15, bf16[1024,928]{1,0:T(8,128)(2,1)} %all-gather.2.cloned.1.call-done), kind=kOutput, calls=%fused_computation.9 | convolution fusion | flops 443509760 | bytes 3667456 | tf_op jit(solution)/shard_map/dot_general | solution.py:24
  253.2 35.3 %reduce-scatter.5.cloned.1.call-done = f32[64,232]{1,0:T(8,128)} async-done(((f32[1024,232]{1,0:T(8,128)}), f32[64,232]{1,0:T(8,128)}) %reduce-scatter.5.cloned.1.call-update) | async-done | bytes 59408 | tf_op jit(solution)/shard_map/reduce_scatter | solution.py:47
  288.5 1.5 convert_element_type.25
  (6 shorter events, 0.0 us)
Async XLA Ops:
  8.0 97.7 %copy-start = (bf16[464,464]{1,0:T(8,128)(2,1)S(1)}, bf16[464,464]{1,0:T(8,128)(2,1)}, u32[]{:S(2)}) copy-start(bf16[464,464]{1,0:T(8,128)(2,1)} %param.12) | copy-start | bytes 1291780
  8.0 172.8 %all-gather.2.cloned.1.call-start = ((), (), s32[]{:S(2)}) async-start(), calls=%async_computation.3 | async-start | bytes 2162688 | tf_op jit(solution)/shard_map/all_gather | solution.py:41
  8.7 239.4 %reduce-scatter.3.cloned.1.call-start = ((), (), s32[]{:S(2)}) async-start(), calls=%async_computation.2 | async-start | bytes 2228224 | tf_op jit(solution)/shard_map/reduce_scatter | solution.py:46
  105.7 75.1 %copy-start.1 = (bf16[232,928]{1,0:T(8,128)(2,1)S(1)}, bf16[232,928]{1,0:T(8,128)(2,1)}, u32[]{:S(2)}) copy-start(bf16[232,928]{1,0:T(8,128)(2,1)} %param.14) | copy-start | bytes 1291780
  107.8 76.3 %copy-start.3 = (bf16[64,232]{1,0:T(8,128)(2,1)S(1)}, bf16[64,232]{1,0:T(8,128)(2,1)}, u32[]{:S(2)}) copy-start(bf16[64,232]{1,0:T(8,128)(2,1)} %param.9) | copy-start | bytes 89092
  107.8 102.1 %copy-start.2 = (bf16[64,464]{1,0:T(8,128)(2,1)S(1)}, bf16[64,464]{1,0:T(8,128)(2,1)}, u32[]{:S(2)}) copy-start(bf16[64,464]{1,0:T(8,128)(2,1)} %param.8) | copy-start | bytes 178180
  107.8 180.7 %reduce-scatter.5.cloned.1.call-start = ((), (), s32[]{:S(2)}) async-start(), calls=%async_computation.4 | async-start | bytes 1114112 | tf_op jit(solution)/shard_map/reduce_scatter | solution.py:47
  184.1 62.3 %copy-start.4 = (bf16[464,464]{1,0:T(8,128)(2,1)S(1)}, bf16[464,464]{1,0:T(8,128)(2,1)}, u32[]{:S(2)}) copy-start(bf16[464,464]{1,0:T(8,128)(2,1)} %param.13) | copy-start | bytes 1291780
  246.4 3.4 %copy-start.5 = (bf16[232,928]{1,0:T(8,128)(2,1)S(1)}, bf16[232,928]{1,0:T(8,128)(2,1)}, u32[]{:S(2)}) copy-start(bf16[232,928]{1,0:T(8,128)(2,1)} %param.15) | copy-start | bytes 1291780
Sparse Core Ops, SparseCore 0:
  10.9 169.7 all-gather.1
Sparse Core Ops, SparseCore 1:
  107.9 91.0 reduce-scatter.2
  203.4 85.0 reduce-scatter.4
where the time goes:
time: 298 us; the launch traced here: 297 us
  blocking collectives  159 us (53%)
  waiting for transfers between devices  109 us (37%)
  between operations  15.5 us (5%)
  matrix products  10.6 us (4%)
  other arithmetic  3 us (1%)
    all_gather x1, blocking collectives, on_device(): lax.all_gather(query_grad, ('gy', 'gz'), axis=0, tiled=True)  96.9 us
    all_gather x1, waiting for transfers between devices, on_device(): lax.all_gather(output_grad, ('gy', 'gz'), axis=0, tiled=True)  72.9 us
    all_gather x1, blocking collectives, on_device(): lax.all_gather(block_input, 'gx', axis=0, tiled=True)  36.5 us
    reduce_scatter x1, waiting for transfers between devices, on_device(): lax.psum_scatter(output_term, 'gx', scatter_dimension=0, tiled=True)  35.3 us
    all_gather x1, blocking collectives, on_device(): lax.all_gather(context, 'gx', axis=0, tiled=True)  25.7 us
  transfers between devices with their start and end apart: 3, of which 2 were waited for; matrix products, arithmetic and copies ran while one was open for 4% of the time, Pallas kernels for 0%

commit v1 on v0

v1 whole, which is shorter than its diff:
```python
import math

import jax
import jax.numpy as jnp
from jax import lax
from jax.sharding import Mesh, PartitionSpec as P

GX, GYZ = ("yh", "x", "core"), ("z", "yl")
SWAP = [(0, 1), (1, 0)]
PAD = 512


def lion_step(gradient, moment):
    held = moment.astype(jnp.float32)
    blended = 0.9 * held + 0.1 * gradient
    direction = blended / jnp.sqrt(blended * blended + 0.01)
    updated = 0.99 * held + 0.01 * gradient
    return (direction.astype(jnp.bfloat16), updated.astype(jnp.bfloat16))


def times_transposed(left, right):
    return lax.dot_general(
        left, right, (((1,), (1,)), ((), ())), preferred_element_type=jnp.float32
    )


def rows_product(left, right):
    return lax.dot_general(
        left, right, (((0,), (0,)), ((), ())), preferred_element_type=jnp.float32
    )


def side_by_side(left, right):
    gap = jnp.zeros((left.shape[0], PAD - left.shape[1]), left.dtype)
    return jnp.concatenate([left, gap, right], axis=1)


def in_order(index, mine, theirs, axis):
    first = jnp.where(index == 0, mine, theirs)
    second = jnp.where(index == 0, theirs, mine)
    return jnp.stack([first, second], axis=axis)


def reduce_scatter(grads, weight, core):
    tokens, width = grads.shape
    chips = tokens // 128
    by_core = grads.reshape(chips, 2, 64, width)
    theirs = lax.dynamic_index_in_dim(by_core, 1 - core, 1, keepdims=False)
    mine = lax.dynamic_index_in_dim(by_core, core, 1, keepdims=False)
    sent = times_transposed(theirs.reshape(-1, width), weight)
    kept = times_transposed(mine.reshape(-1, width), weight)
    pair = kept + lax.ppermute(sent, "core", SWAP)
    parts = lax.all_to_all(
        pair.reshape(chips, 64, -1), ("yh", "x"), 0, 0, tiled=True
    )
    return jnp.sum(parts, axis=0).astype(jnp.bfloat16)


def on_device(
    block_input,
    context,
    query_grad,
    output_grad,
    query_weight,
    query_moment,
    output_weight,
    output_moment,
):
    core, yh = lax.axis_index("core"), lax.axis_index("yh")
    inputs = side_by_side(block_input, context)
    inputs = in_order(yh, inputs, lax.ppermute(inputs, "yh", SWAP), 0)
    grads = lax.all_gather(
        side_by_side(query_grad, output_grad), "yl", axis=0, tiled=True
    )
    output_all = lax.all_gather(grads[:, PAD:], "z", axis=0, tiled=True)
    query_all = lax.all_gather(
        grads[:, : query_grad.shape[1]], "z", axis=0, tiled=True
    )
    inputs = lax.all_to_all(
        jnp.broadcast_to(inputs[None], (4,) + inputs.shape), "x", 0, 0, tiled=True
    )
    inputs = jnp.swapaxes(inputs, 0, 1)
    inputs = in_order(core, inputs, lax.ppermute(inputs, "core", SWAP), 2)
    inputs = inputs.reshape(-1, inputs.shape[-1])
    input_all, context_all = inputs[:, : block_input.shape[1]], inputs[:, PAD:]

    input_grad = reduce_scatter(query_all, query_weight, core)
    context_grad = reduce_scatter(output_all, output_weight, core)
    norm_factor = 1.0 / math.sqrt(float(query_all.shape[0]))
    query_step, query_momentum = lion_step(
        rows_product(input_all, query_all) * norm_factor, query_moment
    )
    output_step, output_momentum = lion_step(
        rows_product(context_all, output_all) * norm_factor, output_moment
    )
    return (
        input_grad,
        context_grad,
        query_step,
        query_momentum,
        output_step,
        output_momentum,
    )


def solution(mesh):
    split = Mesh(mesh.devices.reshape(2, 4, 2, 8, 4), GX + GYZ)
    rows, columns = P(GX, GYZ), P(GYZ, GX)
    return jax.shard_map(
        on_device,
        mesh=split,
        in_specs=(rows, rows) + (columns,) * 6,
        out_specs=(rows, rows) + (columns,) * 4,
        check_vma=False,
    )
```

time: 298 us -> 157 us (0.53)
  the two profiles are of different devices: /device:TPU:2 before, /device:TPU:16 now
where the time goes in v1:
time: 157 us; the launch traced here: 156 us
  blocking collectives  47.4 us (30%)
  waiting for transfers between devices  34.4 us (22%)
  starting transfers between devices  30.6 us (19%)
  between operations  14.2 us (9%)
  matrix products  12 us (8%)
  local copies, waits for them, and re-layouts  10.9 us (7%)
  other arithmetic  6.38 us (4%)
    all_gather x1, blocking collectives, on_device(): lax.all_gather(grads[:, :query_grad.shape[1]], 'z', axis=0, tiled=True)  29.2 us
    all_to_all x2, waiting for transfers between devices, reduce_scatter(): lax.all_to_all(pair.reshape(chips, 64, -1), ('yh', 'x'), 0, 0, tiled=True)  20.6 us
    all_gather x1, blocking collectives, on_device(): lax.all_gather(side_by_side(query_grad, output_grad), 'yl', axis=0, tiled...  18.1 us
    all_to_all x2, starting transfers between devices, reduce_scatter(): lax.all_to_all(pair.reshape(chips, 64, -1), ('yh', 'x'), 0, 0, tiled=True)  11.7 us
    ppermute x1, starting transfers between devices, on_device(): inputs = in_order(yh, inputs, lax.ppermute(inputs, 'yh', SWAP), 0)  8.3 us
    all_to_all x1, waiting for transfers between devices, on_device(): lax.all_to_all(jnp.broadcast_to(inputs[None], (4,) + inputs.shape), 'x',...  8.17 us
    dot_general x4, matrix products, times_transposed(): lax.dot_general(left, right, (((1,), (1,)), ((), ())), preferred_element_...  6.71 us
    ppermute x1, waiting for transfers between devices, on_device(): inputs = in_order(yh, inputs, lax.ppermute(inputs, 'yh', SWAP), 0)  5.59 us
  transfers between devices with their start and end apart: 8, of which 4 were waited for; matrix products, arithmetic and copies ran while one was open for 15% of the time, Pallas kernels for 0%

profile of v1, /device:TPU:16, one launch (start us, length us, event | category | flops | bytes accessed | tf_op | source)
XLA Modules:
  0.0 155.9 jit_solution(14771062825405673659)
XLA Ops:
  8.2 18.1 %all_gather.9 = bf16[128,1440]{1,0:T(8,128)(2,1)S(1)} all-gather(bf16[32,1440]{1,0:T(8,128)(2,1)S(1)} %concatenate.6), channel_id=1, replica_groups=mesh['yh'=2,'x'=4,'core'=2,'z'=8,'yl'=4] {'yl'}, dimensions={0}, use_global_device_ids=true | all-gather | bytes 460800 | tf_op jit(solution)/shard_map/all_gather | solution.py:72
  27.1 29.2 %all_gather.10 = bf16[1024,464]{1,0:T(8,128)(2,1)S(1)} all-gather(bf16[128,464]{1,0:T(8,128)(2,1)S(1)} %slice.16), channel_id=1, replica_groups=mesh['yh'=2,'x'=4,'core'=2,'z'=8,'yl'=4] {'z'}, dimensions={0}, use_global_device_ids=true | all-gather | bytes 1069056 | tf_op jit(solution)/shard_map/all_gather | solution.py:76
  57.3 1.4 fusion.10
  58.6 1.9 %collective-permute-start = (f32[512,464]{0,1:T(8,128)}, f32[512,464]{0,1:T(8,128)S(1)}, u32[]{:S(2)}, u32[]{:S(2)}) collective-permute-start(f32[512,464]{0,1:T(8,128)} %fusion.10), channel_id=1, source_target_pairs={{0,32},{32,0},{1,33},{33,1},{2,34},{34,2},{3,35},{35,3},{4,36},{36... | collective-permute-start | bytes 2850824 | tf_op jit(solution)/shard_map/ppermute | solution.py:52
  60.7 8.3 %collective-permute-start.2 = (bf16[64,744]{1,0:T(8,128)(2,1)S(1)}, bf16[64,744]{1,0:T(8,128)(2,1)S(1)}, u32[]{:S(2)}, u32[]{:S(2)}) collective-permute-start(bf16[64,744]{1,0:T(8,128)(2,1)S(1)} %pad_maximum_fusion.2), channel_id=1, source_target_pairs={{0,256},{256,0},{1,257},{257,1},{2,258},{258,2},{3,259},{259,3},{4... | collective-permute-start | bytes 285704 | tf_op jit(solution)/shard_map/ppermute | solution.py:71
  69.0 5.6 %collective-permute-done.2 = bf16[64,744]{1,0:T(8,128)(2,1)S(1)} collective-permute-done((bf16[64,744]{1,0:T(8,128)(2,1)S(1)}, bf16[64,744]{1,0:T(8,128)(2,1)S(1)}, u32[]{:S(2)}, u32[]{:S(2)}) %collective-permute-start.2) | collective-permute-done | bytes 95264 | tf_op jit(solution)/shard_map/ppermute | solution.py:71
  75.6 4.3 %all-to-all-start.2 = ((bf16[4,2,64,744]{3,2,1,0:T(8,128)(2,1)}), bf16[4,2,64,744]{3,2,1,0:T(8,128)(2,1)S(1)}, u32[]{:S(2)}, u32[]{:S(2)}) async-start(bf16[4,2,64,744]{3,2,1,0:T(8,128)(2,1)} %broadcast_in_dim.14), calls=%async_computation.2 | async-start | bytes 1572864 | tf_op jit(solution)/shard_map/all_to_all | solution.py:79
  80.8 1.8 %convolution_add_fusion = f32[512,464]{0,1:T(8,128)S(1)} fusion(f32[512,464]{0,1:T(8,128)} %copy-done.5, bf16[512,464]{1,0:T(8,128)(2,1)} %bitcast.36, bf16[464,464]{1,0:T(8,128)(2,1)S(1)} %copy-done), kind=kOutput, calls=%fused_computation.1 | convolution fusion | flops 220700672 | bytes 2806272 | tf_op jit(solution)/shard_map/dot_general | solution.py:22
  82.6 1.3 copy.17
  83.9 8.2 %all-to-all-done.2 = bf16[4,2,64,744]{3,2,1,0:T(8,128)(2,1)S(1)} async-done(((bf16[4,2,64,744]{3,2,1,0:T(8,128)(2,1)}), bf16[4,2,64,744]{3,2,1,0:T(8,128)(2,1)S(1)}, u32[]{:S(2)}, u32[]{:S(2)}) %all-to-all-start.2) | async-done | bytes 761888 | tf_op jit(solution)/shard_map/all_to_all | solution.py:79
  92.1 7.3 %all-to-all-start = ((f32[8,64,464]{2,1,0:T(8,128)}), f32[8,64,464]{2,1,0:T(8,128)}, u32[]{:S(2)}, u32[]{:S(2)}) async-start(f32[8,64,464]{2,1,0:T(8,128)} %bitcast.3), calls=%async_computation | async-start | bytes 2097152 | tf_op jit(solution)/shard_map/all_to_all | solution.py:53
  99.4 1.9 %collective-permute-start.3 = (bf16[2,4,64,744]{3,2,0,1:T(8,128)(2,1)S(1)}, bf16[2,4,64,744]{3,2,0,1:T(8,128)(2,1)}, u32[]{:S(2)}, u32[]{:S(2)}) collective-permute-start(bf16[2,4,64,744]{3,2,0,1:T(8,128)(2,1)S(1)} %bitcast.33), channel_id=1, source_target_pairs={{0,32},{32,0},{1,33},{33,1},{2,34},{34,2},{3,35},{35,3},{4,36},{36... | collective-permute-start | bytes 2285576 | tf_op jit(solution)/shard_map/ppermute | solution.py:83
  101.4 1.8 %constant_dynamic-slice_fusion.1 = (bf16[8,1,64,928]{3,2,1,0:T(8,128)(2,1)S(1)}, bf16[8,1,64,928]{3,2,1,0:T(8,128)(2,1)S(1)}) fusion(bf16[8,2,64,928]{3,2,1,0:T(8,128)(2,1)} %bitcast.34, s32[]{:T(128)S(6)} %select_n.34, s32[]{:T(128)S(6)} %select_n.35), kind=kLoop, calls=%fused_computation.26 | loop fusion | bytes 3801096 | tf_op jit(solution)/shard_map/jit(dynamic_index_in_dim)/dynamic_slice | solution.py:49
  104.5 2.4 %collective-permute-start.1 = (f32[512,232]{0,1:T(8,128)}, f32[512,232]{0,1:T(8,128)}, u32[]{:S(2)}, u32[]{:S(2)}) collective-permute-start(f32[512,232]{0,1:T(8,128)} %fusion.11), channel_id=1, source_target_pairs={{0,32},{32,0},{1,33},{33,1},{2,34},{34,2},{3,35},{35,3},{4,36},{36... | collective-permute-start | bytes 1425416 | tf_op jit(solution)/shard_map/ppermute | solution.py:52
  106.9 2.5 %select_bitcast_fusion.1 = (bf16[2,4,1,64,744]{4,3,0,1,2:T(8,128)(2,1)}, bf16[2,4,1,64,744]{4,3,0,1,2:T(8,128)(2,1)}) fusion(bf16[2,4,64,744]{3,2,0,1:T(8,128)(2,1)} %collective-permute-done.3, pred[]{:T(512)S(6)} %eq.8, bf16[4,2,64,744]{3,2,1,0:T(8,128)(2,1)S(1)} %all-to-all-done.2), kind=kLoop, calls=%fused_computation.18 | loop fusion | flops 761856 | bytes 3047425 | tf_op jit(solution)/shard_map/stack | solution.py:41
  109.4 2.3 %convolution_add_fusion.1 = f32[512,232]{0,1:T(8,128)} fusion(f32[512,232]{0,1:T(8,128)} %collective-permute-done.1, bf16[512,928]{1,0:T(8,128)(2,1)S(1)} %bitcast.30, bf16[232,928]{1,0:T(8,128)(2,1)S(1)} %copy-done.4), kind=kOutput, calls=%fused_computation.2 | convolution fusion | flops 220581888 | bytes 2331136 | tf_op jit(solution)/shard_map/dot_general | solution.py:22
  111.7 2.1 %copy.18 = f32[512,232]{1,0:T(8,128)} copy(f32[512,232]{0,1:T(8,128)} %convolution_add_fusion.1) | data formatting | bytes 950272 | tf_op jit(solution)/shard_map/add | solution.py:52
  113.8 12.7 %all-to-all-done = f32[8,64,464]{2,1,0:T(8,128)} async-done(((f32[8,64,464]{2,1,0:T(8,128)}), f32[8,64,464]{2,1,0:T(8,128)}, u32[]{:S(2)}, u32[]{:S(2)}) %all-to-all-start) | async-done | bytes 950304 | tf_op jit(solution)/shard_map/all_to_all | solution.py:53
  126.6 4.4 %all-to-all-start.1 = ((f32[8,64,232]{2,1,0:T(8,128)}), f32[8,64,232]{2,1,0:T(8,128)}, u32[]{:S(2)}, u32[]{:S(2)}) async-start(f32[8,64,232]{2,1,0:T(8,128)} %bitcast.35), calls=%async_computation.1 | async-start | bytes 1048576 | tf_op jit(solution)/shard_map/all_to_all | solution.py:53
  132.2 1.8 %fusion.4 = (bf16[464,464]{1,0:T(8,128)(2,1)}, bf16[464,464]{1,0:T(8,128)(2,1)}) fusion(bf16[464,464]{1,0:T(8,128)(2,1)S(1)} %copy-done.8, bf16[1024,464]{1,0:T(8,128)(2,1)S(1)} %all_gather.10, bf16[1024,744]{1,0:T(8,128)(2,1)S(1)} %bitcast.38), kind=kOutput, calls=%fused_computation.11 | convolution fusion | flops 443509760 | bytes 3433472 | tf_op jit(solution)/shard_map/dot_general | solution.py:28
  134.0 2.0 %reduce_sum.18 = bf16[64,464]{1,0:T(8,128)(2,1)} reduce(f32[8,64,464]{2,1,0:T(8,128)} %all-to-all-done, f32[]{:T(128)} %constant.46.clone.1), dimensions={0}, to_apply=%region_0.1 | reduce | flops 207872 | bytes 1009668 | tf_op jit(solution)/shard_map/reduce_sum | solution.py:56
  136.0 3.5 %fusion.7 = (bf16[232,928]{1,0:T(8,128)(2,1)}, bf16[232,928]{1,0:T(8,128)(2,1)}) fusion(bf16[232,928]{1,0:T(8,128)(2,1)} %param.15, bf16[1024,928]{1,0:T(8,128)(2,1)} %all-gather.2.cloned.1.call-done, bf16[1024,744]{1,0:T(8,128)(2,1)S(1)} %bitcast.39), kind=kOutput, calls=%fused_computation.14 | convolution fusion | flops 443509760 | bytes 3716608 | tf_op jit(solution)/shard_map/dot_general | solution.py:28
  139.5 7.8 %all-to-all-done.1 = f32[8,64,232]{2,1,0:T(8,128)} async-done(((f32[8,64,232]{2,1,0:T(8,128)}), f32[8,64,232]{2,1,0:T(8,128)}, u32[]{:S(2)}, u32[]{:S(2)}) %all-to-all-start.1) | async-done | bytes 475168 | tf_op jit(solution)/shard_map/all_to_all | solution.py:53
  147.3 1.7 %reduce_sum.19 = bf16[64,232]{1,0:T(8,128)(2,1)} reduce(f32[8,64,232]{2,1,0:T(8,128)} %all-to-all-done.1, f32[]{:T(128)} %constant.46.clone.1), dimensions={0}, to_apply=%region_1.2 | reduce | flops 103936 | bytes 504836 | tf_op jit(solution)/shard_map/reduce_sum | solution.py:56
  (38 shorter events, 7.2 us)
Async XLA Ops:
  7.2 50.1 %copy-start = (bf16[464,464]{1,0:T(8,128)(2,1)S(1)}, bf16[464,464]{1,0:T(8,128)(2,1)}, u32[]{:S(2)}) copy-start(bf16[464,464]{1,0:T(8,128)(2,1)} %param.12) | copy-start | bytes 1291780
  7.2 94.2 %all-gather.2.cloned.1.call-start = ((), (), s32[]{:S(2)}) async-start(), calls=%async_computation.3 | async-start | bytes 2359296 | tf_op jit(solution)/shard_map/all_gather | solution.py:75
  56.4 4.3 %copy-start.6 = (bf16[64,464]{1,0:T(8,128)(2,1)S(1)}, bf16[64,464]{1,0:T(8,128)(2,1)}, u32[]{:S(2)}) copy-start(bf16[64,464]{1,0:T(8,128)(2,1)} %param.8) | copy-start | bytes 178180
  56.4 4.3 %copy-start.7 = (bf16[64,232]{1,0:T(8,128)(2,1)S(1)}, bf16[64,232]{1,0:T(8,128)(2,1)}, u32[]{:S(2)}) copy-start(bf16[64,232]{1,0:T(8,128)(2,1)} %param.9) | copy-start | bytes 89092
  58.6 21.3 %collective-permute-start = (f32[512,464]{0,1:T(8,128)}, f32[512,464]{0,1:T(8,128)S(1)}, u32[]{:S(2)}, u32[]{:S(2)}) collective-permute-start(f32[512,464]{0,1:T(8,128)} %fusion.10), channel_id=1, source_target_pairs={{0,32},{32,0},{1,33},{33,1},{2,34},{34,2},{3,35},{35,3},{4,36},{36... | collective-permute-start | bytes 2850824 | tf_op jit(solution)/shard_map/ppermute | solution.py:52
  60.7 13.9 %collective-permute-start.2 = (bf16[64,744]{1,0:T(8,128)(2,1)S(1)}, bf16[64,744]{1,0:T(8,128)(2,1)S(1)}, u32[]{:S(2)}, u32[]{:S(2)}) collective-permute-start(bf16[64,744]{1,0:T(8,128)(2,1)S(1)} %pad_maximum_fusion.2), channel_id=1, source_target_pairs={{0,256},{256,0},{1,257},{257,1},{2,258},{258,2},{3,259},{259,3},{4... | collective-permute-start | bytes 285704 | tf_op jit(solution)/shard_map/ppermute | solution.py:71
  75.6 16.5 %all-to-all-start.2 = ((bf16[4,2,64,744]{3,2,1,0:T(8,128)(2,1)}), bf16[4,2,64,744]{3,2,1,0:T(8,128)(2,1)S(1)}, u32[]{:S(2)}, u32[]{:S(2)}) async-start(bf16[4,2,64,744]{3,2,1,0:T(8,128)(2,1)} %broadcast_in_dim.14), calls=%async_computation.2 | async-start | bytes 1572864 | tf_op jit(solution)/shard_map/all_to_all | solution.py:79
  79.9 0.9 copy-start.5
  92.1 34.5 %all-to-all-start = ((f32[8,64,464]{2,1,0:T(8,128)}), f32[8,64,464]{2,1,0:T(8,128)}, u32[]{:S(2)}, u32[]{:S(2)}) async-start(f32[8,64,464]{2,1,0:T(8,128)} %bitcast.3), calls=%async_computation | async-start | bytes 2097152 | tf_op jit(solution)/shard_map/all_to_all | solution.py:53
  99.4 7.5 %collective-permute-start.3 = (bf16[2,4,64,744]{3,2,0,1:T(8,128)(2,1)S(1)}, bf16[2,4,64,744]{3,2,0,1:T(8,128)(2,1)}, u32[]{:S(2)}, u32[]{:S(2)}) collective-permute-start(bf16[2,4,64,744]{3,2,0,1:T(8,128)(2,1)S(1)} %bitcast.33), channel_id=1, source_target_pairs={{0,32},{32,0},{1,33},{33,1},{2,34},{34,2},{3,35},{35,3},{4,36},{36... | collective-permute-start | bytes 2285576 | tf_op jit(solution)/shard_map/ppermute | solution.py:83
  101.4 1.9 %copy-start.3 = (bf16[232,928]{1,0:T(8,128)(2,1)S(1)}, bf16[232,928]{1,0:T(8,128)(2,1)}, u32[]{:S(2)}) copy-start(bf16[232,928]{1,0:T(8,128)(2,1)} %param.14) | copy-start | bytes 1291780
  104.5 4.9 %collective-permute-start.1 = (f32[512,232]{0,1:T(8,128)}, f32[512,232]{0,1:T(8,128)}, u32[]{:S(2)}, u32[]{:S(2)}) collective-permute-start(f32[512,232]{0,1:T(8,128)} %fusion.11), channel_id=1, source_target_pairs={{0,32},{32,0},{1,33},{33,1},{2,34},{34,2},{3,35},{35,3},{4,36},{36... | collective-permute-start | bytes 1425416 | tf_op jit(solution)/shard_map/ppermute | solution.py:52
  106.9 2.5 %copy-start.4 = (bf16[232,928]{1,0:T(8,128)(2,1)S(1)}, bf16[232,928]{1,0:T(8,128)(2,1)}, u32[]{:S(2)}) copy-start(bf16[232,928]{1,0:T(8,128)(2,1)} %param.14) | copy-start | bytes 1291780
  111.7 19.3 %copy-start.1 = (bf16[2,4,1,64,744]{4,3,0,1,2:T(8,128)(2,1)S(1)}, bf16[2,4,1,64,744]{4,3,0,1,2:T(8,128)(2,1)}, u32[]{:S(2)}) copy-start(bf16[2,4,1,64,744]{4,3,0,1,2:T(8,128)(2,1)} %get-tuple-element.8) | copy-start | bytes 2285572
  111.7 19.3 %copy-start.2 = (bf16[2,4,1,64,744]{4,3,0,1,2:T(8,128)(2,1)S(1)}, bf16[2,4,1,64,744]{4,3,0,1,2:T(8,128)(2,1)}, u32[]{:S(2)}) copy-start(bf16[2,4,1,64,744]{4,3,0,1,2:T(8,128)(2,1)} %get-tuple-element.9) | copy-start | bytes 2285572
  126.6 20.7 %all-to-all-start.1 = ((f32[8,64,232]{2,1,0:T(8,128)}), f32[8,64,232]{2,1,0:T(8,128)}, u32[]{:S(2)}, u32[]{:S(2)}) async-start(f32[8,64,232]{2,1,0:T(8,128)} %bitcast.35), calls=%async_computation.1 | async-start | bytes 1048576 | tf_op jit(solution)/shard_map/all_to_all | solution.py:53
  131.2 1.0 copy-start.8
Sparse Core Ops, SparseCore 0:
  27.2 47.2 all-gather.1

commit v2 on v1

v2 whole, which is shorter than its diff:
```python
import functools
import math

import jax
import jax.numpy as jnp
from jax import lax
from jax.experimental import pallas as pl
from jax.experimental.pallas import tpu as pltpu
from jax.sharding import Mesh, PartitionSpec as P

GX, GYZ = ("yh", "x", "core"), ("z", "yl")
SWAP = [(0, 1), (1, 0)]
PAD = 512
MIB = 2**20


def times_transposed(left, right):
    return lax.dot_general(
        left, right, (((1,), (1,)), ((), ())), preferred_element_type=jnp.float32
    )


def rows_product(left, right):
    return lax.dot_general(
        left, right, (((0,), (0,)), ((), ())), preferred_element_type=jnp.float32
    )


def lanes(columns):
    return -(-columns // 128) * 128


def side_by_side(left, right):
    gap = jnp.zeros((left.shape[0], PAD - left.shape[1]), left.dtype)
    return jnp.concatenate([left, gap, right], axis=1)


def call(kernel, out_shapes, out_specs, in_specs, pick, *operands, flops=0):
    whole = lambda array: pl.BlockSpec(array.shape, lambda i, pick: (0,) * array.ndim)
    moved = sum(o.size * o.dtype.itemsize for o in operands)
    return pl.pallas_call(
        kernel,
        grid_spec=pltpu.PrefetchScalarGridSpec(
            num_scalar_prefetch=1,
            grid=(1,),
            in_specs=[spec or whole(o) for spec, o in zip(in_specs, operands)],
            out_specs=[spec or whole(o) for spec, o in zip(out_specs, out_shapes)],
        ),
        out_shape=out_shapes,
        compiler_params=pltpu.CompilerParams(vmem_limit_bytes=20 * MIB),
        cost_estimate=pl.CostEstimate(
            flops=flops, bytes_accessed=moved, transcendentals=0
        ),
    )(pick, *operands)


def product_kernel(x_first, pick, grads, weight, *rest):
    out, received = rest[-1], rest[:-1]
    product = times_transposed(grads[...].reshape(-1, grads.shape[-1]), weight[...])
    features = product.shape[1]
    if received:
        product = product + received[0][:, :features]
    if x_first:
        blocks = product.reshape(2, 4, 64, features)
        for yh in range(2):
            for x in range(4):
                out[x, yh, :, :features] = blocks[yh, x]
        out[:, :, :, features:] = jnp.zeros(
            (4, 2, 64, out.shape[-1] - features), jnp.float32
        )
    else:
        out[:, :features] = product
        out[:, features:] = jnp.zeros(
            (out.shape[0], out.shape[1] - features), jnp.float32
        )


def token_half(half, grads, weight, *received, x_first=False):
    tokens, width = grads.shape
    chips, columns = tokens // 128, lanes(weight.shape[0])
    shape = (4, 2, 64, columns) if x_first else (chips * 64, columns)
    return call(
        functools.partial(product_kernel, x_first),
        [jax.ShapeDtypeStruct(shape, jnp.float32)],
        [None],
        [pl.BlockSpec((chips, 1, 64, width), lambda i, pick: (0, pick[0], 0, 0)), None]
        + [None] * len(received),
        half.reshape(1),
        grads.reshape(chips, 2, 64, width),
        weight,
        *received,
        flops=2 * chips * 64 * columns * width,
    )[0]


def sum_along_x_kernel(pick, near_parts, far_parts, near, far):
    near[...] = jnp.sum(near_parts[...], axis=(0, 1))
    far[...] = jnp.sum(far_parts[...], axis=(0, 1))


def sum_along_x(yh, parts):
    block = (4, 1, 64, parts.shape[-1])
    shape = jax.ShapeDtypeStruct((64, parts.shape[-1]), jnp.float32)
    return call(
        sum_along_x_kernel,
        [shape] * 2,
        [None] * 2,
        [
            pl.BlockSpec(block, lambda i, pick: (0, pick[0], 0, 0)),
            pl.BlockSpec(block, lambda i, pick: (0, 1 - pick[0], 0, 0)),
        ],
        yh.reshape(1),
        parts,
        parts,
    )


def total_kernel(pick, parts, out):
    features = out.shape[-1]
    out[...] = jnp.sum(parts[...], axis=0)[:, :features].astype(jnp.bfloat16)


def total(parts, features):
    return call(
        total_kernel,
        [jax.ShapeDtypeStruct((parts.shape[1], features), jnp.bfloat16)],
        [None],
        [None],
        jnp.zeros((1,), jnp.int32),
        parts,
    )[0]


def momentum_kernel(
    first, pick, inputs, inputs_theirs, grads, grads_theirs, moment, step, momentum
):
    rows = pl.ds(first, moment.shape[0])
    tokens = grads.shape[0] * grads.shape[2]
    width = grads.shape[-1]
    gradient = rows_product(
        inputs[..., rows].reshape(tokens, -1), grads[...].reshape(tokens, width)
    ) + rows_product(
        inputs_theirs[..., rows].reshape(tokens, -1),
        grads_theirs[...].reshape(tokens, width),
    )
    gradient = gradient * (1.0 / math.sqrt(float(2 * tokens)))
    held = moment[...].astype(jnp.float32)
    blended = 0.9 * held + 0.1 * gradient
    step[...] = (blended / jnp.sqrt(blended * blended + 0.01)).astype(jnp.bfloat16)
    momentum[...] = (0.99 * held + 0.01 * gradient).astype(jnp.bfloat16)


def momentum_step(core, inputs, inputs_theirs, first, grads, moment):
    tokens, width = grads.shape
    grads = grads.reshape(tokens // 128, 2, 64, width)
    block = (tokens // 128, 1, 64, width)
    return call(
        functools.partial(momentum_kernel, first),
        [jax.ShapeDtypeStruct(moment.shape, jnp.bfloat16)] * 2,
        [None] * 2,
        [
            None,
            None,
            pl.BlockSpec(block, lambda i, pick: (0, pick[0], 0, 0)),
            pl.BlockSpec(block, lambda i, pick: (0, 1 - pick[0], 0, 0)),
            None,
        ],
        core.reshape(1),
        inputs,
        inputs_theirs,
        grads,
        grads,
        moment,
        flops=2 * tokens * moment.size,
    )


def on_device(
    block_input,
    context,
    query_grad,
    output_grad,
    query_weight,
    query_moment,
    output_weight,
    output_moment,
):
    core, yh = lax.axis_index("core"), lax.axis_index("yh")
    width = query_grad.shape[1]
    grads = side_by_side(query_grad, output_grad)
    grads = lax.all_gather(grads, "yl", axis=0, tiled=True)
    inputs = side_by_side(block_input, context)
    grads, inputs = lax.optimization_barrier((grads, inputs))
    output_all = lax.all_gather(grads[:, PAD:], "z", axis=0, tiled=True)
    inputs = jnp.broadcast_to(inputs[None], (8,) + inputs.shape)
    inputs = lax.all_to_all(inputs, ("yh", "x"), 0, 0, tiled=True)
    query_all = lax.all_gather(grads[:, :width], "z", axis=0, tiled=True)
    query_all, inputs = lax.optimization_barrier((query_all, inputs))
    query_theirs = token_half(1 - core, query_all, query_weight)
    query_theirs = lax.ppermute(query_theirs, "core", SWAP)
    inputs_theirs = lax.ppermute(inputs, "core", SWAP)
    query_pair = token_half(core, query_all, query_weight, query_theirs, x_first=True)
    query_parts = lax.all_to_all(query_pair, "x", 0, 0, tiled=True)
    output_theirs = token_half(1 - core, output_all, output_weight)
    output_theirs = lax.ppermute(output_theirs, "core", SWAP)
    output_pair = token_half(core, output_all, output_weight, output_theirs)
    query_parts, output_pair = lax.optimization_barrier((query_parts, output_pair))
    output_pair = output_pair.reshape(8, 64, output_pair.shape[-1])
    output_parts = lax.all_to_all(output_pair, ("yh", "x"), 0, 0, tiled=True)
    context_grad = total(output_parts, context.shape[1])
    query_near, query_far = sum_along_x(yh, query_parts)
    query_far = lax.ppermute(query_far, "yh", SWAP)
    input_grad = (query_near + query_far)[:, : block_input.shape[1]]
    input_grad = input_grad.astype(jnp.bfloat16)
    query_step, query_momentum = momentum_step(
        core, inputs, inputs_theirs, 0, query_all, query_moment
    )
    output_step, output_momentum = momentum_step(
        core, inputs, inputs_theirs, PAD, output_all, output_moment
    )
    return (
        input_grad,
        context_grad,
        query_step,
        query_momentum,
        output_step,
        output_momentum,
    )


def solution(mesh):
    split = Mesh(mesh.devices.reshape(2, 4, 2, 8, 4), GX + GYZ)
    rows, columns = P(GX, GYZ), P(GYZ, GX)
    return jax.shard_map(
        on_device,
        mesh=split,
        in_specs=(rows, rows) + (columns,) * 6,
        out_specs=(rows, rows) + (columns,) * 4,
        check_vma=False,
    )
```

time: 157 us -> 135 us (0.86)
  waiting for transfers between devices: 34.4 us -> 18.2 us
  matrix products: 12 us -> 0 us
  Pallas kernels: 0 us -> 9.02 us
  blocking collectives: 47.4 us -> 53.6 us
  other arithmetic: 6.38 us -> 1.53 us
  local copies, waits for them, and re-layouts: 10.9 us -> 6.08 us
    all_to_all x3, waiting for transfers between devices: 28.7 us -> 7.69 us  [the longest x1 7.68 us: on_device(): query_parts = lax.all_to_all(query_pair, 'x', 0, 0, tiled=True)]
    dot_general x6 -> x0, matrix products: 12 us -> none  [the longest x4 6.71 us: times_transposed(): lax.dot_general(left, right, (((1,), (1,)), ((), ())), preferred_element_...]
    pallas_call x0 -> x8, Pallas kernels: none -> 9.02 us  [call(): pl.pallas_call(kernel, grid_spec=pltpu.PrefetchScalarGridSpec(num_scalar_...]
    all_gather x2, blocking collectives: 47.4 us -> 53.6 us  [the longest x1 35.4 us: on_device(): query_all = lax.all_gather(grads[:, :width], 'z', axis=0, tiled=True)]
    ppermute x4, waiting for transfers between devices: 5.6 us -> 10.5 us  [the longest x1 7.88 us: on_device(): query_far = lax.ppermute(query_far, 'yh', SWAP)]
    reduce_sum x2 -> x0, other arithmetic: 3.65 us -> none  [reduce_scatter(): return jnp.sum(parts, axis=0).astype(jnp.bfloat16)]
    add x2 -> x0, local copies, waits for them, and re-layouts: 3.46 us -> none  [reduce_scatter(): pair = kept + lax.ppermute(sent, 'core', SWAP)]
    dynamic_slice x2 -> x0, local copies, waits for them, and re-layouts: 2.73 us -> none  [reduce_scatter(): mine = lax.dynamic_index_in_dim(by_core, core, 1, keepdims=False)]
  transfers between devices with their start and end apart: 8 -> 8, of which waited for: 4 -> 3; matrix products, arithmetic and copies ran while one was open for 15% -> 1% of each run, Pallas kernels for 0% -> 6%
where the time goes in v2:
time: 135 us; the launch traced here: 134 us
  blocking collectives  53.6 us (40%)
  starting transfers between devices  31.2 us (23%)
  waiting for transfers between devices  18.2 us (13%)
  between operations  14.2 us (11%)
  Pallas kernels  9.02 us (7%)
  local copies, waits for them, and re-layouts  6.08 us (5%)
  other arithmetic  1.53 us (1%)
    all_gather x1, blocking collectives, on_device(): query_all = lax.all_gather(grads[:, :width], 'z', axis=0, tiled=True)  35.4 us
    all_gather x1, blocking collectives, on_device(): grads = lax.all_gather(grads, 'yl', axis=0, tiled=True)  18.1 us
    pallas_call x8, Pallas kernels, call(): pl.pallas_call(kernel, grid_spec=pltpu.PrefetchScalarGridSpec(num_scalar_...  9.02 us
    ppermute x1, starting transfers between devices, on_device(): query_far = lax.ppermute(query_far, 'yh', SWAP)  8.09 us
    ppermute x1, waiting for transfers between devices, on_device(): query_far = lax.ppermute(query_far, 'yh', SWAP)  7.88 us
    all_to_all x1, waiting for transfers between devices, on_device(): query_parts = lax.all_to_all(query_pair, 'x', 0, 0, tiled=True)  7.68 us
    all_to_all x1, starting transfers between devices, on_device(): output_parts = lax.all_to_all(output_pair, ('yh', 'x'), 0, 0, tiled=True)  7.4 us
    all_to_all x1, starting transfers between devices, on_device(): query_parts = lax.all_to_all(query_pair, 'x', 0, 0, tiled=True)  4.97 us
  transfers between devices with their start and end apart: 8, of which 3 were waited for; matrix products, arithmetic and copies ran while one was open for 1% of the time, Pallas kernels for 6%

profile of v2, /device:TPU:16, one launch (start us, length us, event | category | flops | bytes accessed | tf_op | source)
XLA Modules:
  0.0 133.9 jit_solution(6032664737540265553)
XLA Ops:
  7.2 0.9 concatenate.6
  8.2 18.1 %all_gather.9 = bf16[128,1440]{1,0:T(8,128)(2,1)S(1)} all-gather(bf16[32,1440]{1,0:T(8,128)(2,1)S(1)} %concatenate.6), channel_id=1, replica_groups=mesh['yh'=2,'x'=4,'core'=2,'z'=8,'yl'=4] {'yl'}, dimensions={0}, use_global_device_ids=true | all-gather | bytes 460800 | tf_op jit(solution)/shard_map/all_gather | solution.py:191
  26.4 0.9 pad_maximum_fusion
  27.3 0.7 slice.11
  28.0 0.9 broadcast_in_dim.14
  29.0 4.5 %all-to-all-start = ((bf16[8,64,744]{2,1,0:T(8,128)(2,1)}), bf16[8,64,744]{2,1,0:T(8,128)(2,1)S(1)}, u32[]{:S(2)}, u32[]{:S(2)}) async-start(bf16[8,64,744]{2,1,0:T(8,128)(2,1)} %broadcast_in_dim.14), calls=%async_computation | async-start | bytes 1572864 | tf_op jit(solution)/shard_map/all_to_all | solution.py:196
  33.5 35.4 %all_gather.10 = bf16[1024,464]{1,0:T(8,128)(2,1)S(1)} all-gather(bf16[128,464]{1,0:T(8,128)(2,1)S(1)} %slice.10), channel_id=1, replica_groups=mesh['yh'=2,'x'=4,'core'=2,'z'=8,'yl'=4] {'z'}, dimensions={0}, use_global_device_ids=true | all-gather | bytes 1069056 | tf_op jit(solution)/shard_map/all_gather | solution.py:197
  69.4 1.9 %collective-permute-start = (f32[512,512]{1,0:T(8,128)S(1)}, f32[512,512]{1,0:T(8,128)S(1)}, u32[]{:S(2)}, u32[]{:S(2)}) collective-permute-start(f32[512,512]{1,0:T(8,128)S(1)} %shard_map.127), channel_id=1, source_target_pairs={{0,32},{32,0},{1,33},{33,1},{2,34},{34,2},{3,35},{35,3},{4,36},{36... | collective-permute-start | bytes 3145736 | tf_op jit(solution)/shard_map/ppermute | solution.py:200
  71.3 2.6 %collective-permute-done.rest_0_ = f32[512,512]{1,0:T(8,128)S(1)} collective-permute-done((f32[512,512]{1,0:T(8,128)S(1)}, f32[512,512]{1,0:T(8,128)S(1)}, u32[]{:S(2)}, u32[]{:S(2)}) %collective-permute-start) | collective-permute-done | bytes 1048608 | tf_op jit(solution)/shard_map/ppermute | solution.py:200
  74.4 1.0 copy-done.2
  75.4 5.0 %all-to-all-start.1 = ((f32[4,2,64,512]{3,2,1,0:T(8,128)}), f32[4,2,64,512]{3,2,1,0:T(8,128)S(1)}, u32[]{:S(2)}, u32[]{:S(2)}) async-start(f32[4,2,64,512]{3,2,1,0:T(8,128)} %copy-done.2), calls=%async_computation.1 | async-start | bytes 2097152 | tf_op jit(solution)/shard_map/all_to_all | solution.py:203
  80.4 1.6 %copy-done = bf16[1024,928]{1,0:T(8,128)(2,1)S(1)} copy-done((bf16[1024,928]{1,0:T(8,128)(2,1)S(1)}, bf16[1024,928]{1,0:T(8,128)(2,1)}, u32[]{:S(2)}) %copy-start) | copy-done | bytes 1900568
  82.4 1.9 %collective-permute-start.1 = (f32[512,256]{1,0:T(8,128)S(1)}, f32[512,256]{1,0:T(8,128)S(1)}, u32[]{:S(2)}, u32[]{:S(2)}) collective-permute-start(f32[512,256]{1,0:T(8,128)S(1)} %shard_map.129), channel_id=1, source_target_pairs={{0,32},{32,0},{1,33},{33,1},{2,34},{34,2},{3,35},{35,3},{4,36},{36... | collective-permute-start | bytes 1572872 | tf_op jit(solution)/shard_map/ppermute | solution.py:205
  84.3 2.4 %collective-permute-start.3 = (bf16[8,64,744]{2,1,0:T(8,128)(2,1)S(1)}, bf16[8,64,744]{2,1,0:T(8,128)(2,1)}, u32[]{:S(2)}, u32[]{:S(2)}) collective-permute-start(bf16[8,64,744]{2,1,0:T(8,128)(2,1)S(1)} %all-to-all-done.inputs), channel_id=1, source_target_pairs={{0,32},{32,0},{1,33},{33,1},{2,34},{34,2},{3,35},{35,3},{4,36},{36... | collective-permute-start | bytes 2285576 | tf_op jit(solution)/shard_map/ppermute | solution.py:201
  86.8 0.5 shard_map.130
  87.3 0.8 copy-done.3
  88.1 7.7 %all-to-all-done.1.near_parts.far_parts = f32[4,2,64,512]{3,2,1,0:T(8,128)S(1)} async-done(((f32[4,2,64,512]{3,2,1,0:T(8,128)}), f32[4,2,64,512]{3,2,1,0:T(8,128)S(1)}, u32[]{:S(2)}, u32[]{:S(2)}) %all-to-all-start.1) | async-done | bytes 1048608 | tf_op jit(solution)/shard_map/all_to_all | solution.py:203
  95.7 7.4 %all-to-all-start.2 = ((f32[8,64,256]{2,1,0:T(8,128)}), f32[8,64,256]{2,1,0:T(8,128)S(1)}, u32[]{:S(2)}, u32[]{:S(2)}) async-start(f32[8,64,256]{2,1,0:T(8,128)} %bitcast.14), calls=%async_computation.2 | async-start | bytes 1048576 | tf_op jit(solution)/shard_map/all_to_all | solution.py:209
  103.2 8.1 %collective-permute-start.2 = (f32[64,512]{1,0:T(8,128)S(1)}, f32[64,512]{1,0:T(8,128)S(1)}, u32[]{:S(2)}, u32[]{:S(2)}) collective-permute-start(f32[64,512]{1,0:T(8,128)S(1)} %get-tuple-element.23), channel_id=1, source_target_pairs={{0,256},{256,0},{1,257},{257,1},{2,258},{258,2},{3,259},{259,3},{4... | collective-permute-start | bytes 393224 | tf_op jit(solution)/shard_map/ppermute | solution.py:212
  111.3 3.3 %shard_map.133 = (bf16[464,464]{1,0:T(8,128)(2,1)}, bf16[464,464]{1,0:T(8,128)(2,1)}) custom-call(s32[1]{0:T(128)} %bitcast.1.pick, bf16[8,64,744]{2,1,0:T(8,128)(2,1)S(1)} %all-to-all-done.inputs, bf16[8,64,744]{2,1,0:T(8,128)(2,1)} %collective-permute-done.3.inputs_theirs, bf16[8,2,64,464]{3,2,1,0:T(8,128)(2,1)S(1)} %bitcast.12, ...), custom_call_target="tpu_custom_call" | custom-call | flops 440926208 | bytes 3854848 | tf_op jit(solution)/shard_map/pallas_call | solution.py:41
  114.6 3.2 %shard_map.134 = (bf16[232,928]{1,0:T(8,128)(2,1)}, bf16[232,928]{1,0:T(8,128)(2,1)}) custom-call(s32[1]{0:T(128)} %bitcast.1.pick, bf16[8,64,744]{2,1,0:T(8,128)(2,1)S(1)} %all-to-all-done.inputs, bf16[8,64,744]{2,1,0:T(8,128)(2,1)} %collective-permute-done.3.inputs_theirs, bf16[8,2,64,928]{3,2,1,0:T(8,128)(2,1)S(1)} %bitcast.8, ...), custom_call_target="tpu_custom_call" | custom-call | flops 440926208 | bytes 5755392 | tf_op jit(solution)/shard_map/pallas_call | solution.py:41
  117.8 7.9 %collective-permute-done.2 = f32[64,512]{1,0:T(8,128)S(1)} collective-permute-done((f32[64,512]{1,0:T(8,128)S(1)}, f32[64,512]{1,0:T(8,128)S(1)}, u32[]{:S(2)}, u32[]{:S(2)}) %collective-permute-start.2) | collective-permute-done | bytes 131104 | tf_op jit(solution)/shard_map/ppermute | solution.py:212
  125.7 0.6 fusion
  126.4 0.6 shard_map.132
  (28 shorter events, 1.6 us)
Async XLA Ops:
  7.2 73.2 %all-gather.2.cloned.1.call-start = ((), (), s32[]{:S(2)}) async-start(), calls=%async_computation.3 | async-start | bytes 2359296 | tf_op jit(solution)/shard_map/all_gather | solution.py:194
  28.0 40.9 %copy-start.5 = (bf16[464,464]{1,0:T(8,128)(2,1)S(1)}, bf16[464,464]{1,0:T(8,128)(2,1)}, u32[]{:S(2)}) copy-start(bf16[464,464]{1,0:T(8,128)(2,1)} %weight.5) | copy-start | bytes 1291780
  29.0 39.9 %all-to-all-start = ((bf16[8,64,744]{2,1,0:T(8,128)(2,1)}), bf16[8,64,744]{2,1,0:T(8,128)(2,1)S(1)}, u32[]{:S(2)}, u32[]{:S(2)}) async-start(bf16[8,64,744]{2,1,0:T(8,128)(2,1)} %broadcast_in_dim.14), calls=%async_computation | async-start | bytes 1572864 | tf_op jit(solution)/shard_map/all_to_all | solution.py:196
  69.4 4.6 %collective-permute-start = (f32[512,512]{1,0:T(8,128)S(1)}, f32[512,512]{1,0:T(8,128)S(1)}, u32[]{:S(2)}, u32[]{:S(2)}) collective-permute-start(f32[512,512]{1,0:T(8,128)S(1)} %shard_map.127), channel_id=1, source_target_pairs={{0,32},{32,0},{1,33},{33,1},{2,34},{34,2},{3,35},{35,3},{4,36},{36... | collective-permute-start | bytes 3145736 | tf_op jit(solution)/shard_map/ppermute | solution.py:200
  73.9 6.4 %copy-start.4 = (bf16[232,928]{1,0:T(8,128)(2,1)S(1)}, bf16[232,928]{1,0:T(8,128)(2,1)}, u32[]{:S(2)}) copy-start(bf16[232,928]{1,0:T(8,128)(2,1)} %weight.7) | copy-start | bytes 1291780
  74.4 1.0 copy-start.2
  75.4 20.4 %all-to-all-start.1 = ((f32[4,2,64,512]{3,2,1,0:T(8,128)}), f32[4,2,64,512]{3,2,1,0:T(8,128)S(1)}, u32[]{:S(2)}, u32[]{:S(2)}) async-start(f32[4,2,64,512]{3,2,1,0:T(8,128)} %copy-done.2), calls=%async_computation.1 | async-start | bytes 2097152 | tf_op jit(solution)/shard_map/all_to_all | solution.py:203
  80.3 1.6 %copy-start = (bf16[1024,928]{1,0:T(8,128)(2,1)S(1)}, bf16[1024,928]{1,0:T(8,128)(2,1)}, u32[]{:S(2)}) copy-start(bf16[1024,928]{1,0:T(8,128)(2,1)} %all-gather.2.cloned.1.call-done) | copy-start | bytes 5701636
  82.4 4.3 %collective-permute-start.1 = (f32[512,256]{1,0:T(8,128)S(1)}, f32[512,256]{1,0:T(8,128)S(1)}, u32[]{:S(2)}, u32[]{:S(2)}) collective-permute-start(f32[512,256]{1,0:T(8,128)S(1)} %shard_map.129), channel_id=1, source_target_pairs={{0,32},{32,0},{1,33},{33,1},{2,34},{34,2},{3,35},{35,3},{4,36},{36... | collective-permute-start | bytes 1572872 | tf_op jit(solution)/shard_map/ppermute | solution.py:205
  84.3 27.0 %collective-permute-start.3 = (bf16[8,64,744]{2,1,0:T(8,128)(2,1)S(1)}, bf16[8,64,744]{2,1,0:T(8,128)(2,1)}, u32[]{:S(2)}, u32[]{:S(2)}) collective-permute-start(bf16[8,64,744]{2,1,0:T(8,128)(2,1)S(1)} %all-to-all-done.inputs), channel_id=1, source_target_pairs={{0,32},{32,0},{1,33},{33,1},{2,34},{34,2},{3,35},{35,3},{4,36},{36... | collective-permute-start | bytes 2285576 | tf_op jit(solution)/shard_map/ppermute | solution.py:201
  87.3 0.8 copy-start.3
  95.7 30.6 %all-to-all-start.2 = ((f32[8,64,256]{2,1,0:T(8,128)}), f32[8,64,256]{2,1,0:T(8,128)S(1)}, u32[]{:S(2)}, u32[]{:S(2)}) async-start(f32[8,64,256]{2,1,0:T(8,128)} %bitcast.14), calls=%async_computation.2 | async-start | bytes 1048576 | tf_op jit(solution)/shard_map/all_to_all | solution.py:209
  103.1 8.2 %copy-start.6 = (bf16[464,464]{1,0:T(8,128)(2,1)S(1)}, bf16[464,464]{1,0:T(8,128)(2,1)}, u32[]{:S(2)}) copy-start(bf16[464,464]{1,0:T(8,128)(2,1)} %moment.2) | copy-start | bytes 1291780
  103.2 11.4 %copy-start.1 = (bf16[1024,928]{1,0:T(8,128)(2,1)S(1)}, bf16[1024,928]{1,0:T(8,128)(2,1)}, u32[]{:S(2)}) copy-start(bf16[1024,928]{1,0:T(8,128)(2,1)} %all-gather.2.cloned.1.call-done) | copy-start | bytes 5701636
  103.2 11.4 %copy-start.7 = (bf16[232,928]{1,0:T(8,128)(2,1)S(1)}, bf16[232,928]{1,0:T(8,128)(2,1)}, u32[]{:S(2)}) copy-start(bf16[232,928]{1,0:T(8,128)(2,1)} %moment.3) | copy-start | bytes 1291780
  103.2 22.5 %collective-permute-start.2 = (f32[64,512]{1,0:T(8,128)S(1)}, f32[64,512]{1,0:T(8,128)S(1)}, u32[]{:S(2)}, u32[]{:S(2)}) collective-permute-start(f32[64,512]{1,0:T(8,128)S(1)} %get-tuple-element.23), channel_id=1, source_target_pairs={{0,256},{256,0},{1,257},{257,1},{2,258},{258,2},{3,259},{259,3},{4... | collective-permute-start | bytes 393224 | tf_op jit(solution)/shard_map/ppermute | solution.py:212
Sparse Core Ops, SparseCore 0:
  28.1 49.5 all-gather.1

commit v3 on v2

v3 whole, which is shorter than its diff:
```python
import functools
import math

import jax
import jax.numpy as jnp
from jax import lax
from jax.experimental import pallas as pl
from jax.experimental.pallas import tpu as pltpu
from jax.sharding import Mesh, PartitionSpec as P

GX, GYZ = ("yh", "x", "core"), ("z", "yl")
SWAP = [(0, 1), (1, 0)]
PAD = 512
MIB = 2**20


def times_transposed(left, right):
    return lax.dot_general(
        left, right, (((1,), (1,)), ((), ())), preferred_element_type=jnp.float32
    )


def rows_product(left, right):
    return lax.dot_general(
        left, right, (((0,), (0,)), ((), ())), preferred_element_type=jnp.float32
    )


def lanes(columns):
    return -(-columns // 128) * 128


def side_by_side(left, right):
    gap = jnp.zeros((left.shape[0], PAD - left.shape[1]), left.dtype)
    return jnp.concatenate([left, gap, right], axis=1)


def call(
    kernel, out_shapes, out_specs, in_specs, pick, *operands, flops=0, scratch=()
):
    whole = lambda array: pl.BlockSpec(array.shape, lambda i, pick: (0,) * array.ndim)
    moved = sum(o.size * o.dtype.itemsize for o in operands)
    return pl.pallas_call(
        kernel,
        grid_spec=pltpu.PrefetchScalarGridSpec(
            num_scalar_prefetch=1,
            grid=(1,),
            scratch_shapes=scratch,
            in_specs=[spec or whole(o) for spec, o in zip(in_specs, operands)],
            out_specs=[spec or whole(o) for spec, o in zip(out_specs, out_shapes)],
        ),
        out_shape=out_shapes,
        compiler_params=pltpu.CompilerParams(vmem_limit_bytes=20 * MIB),
        cost_estimate=pl.CostEstimate(
            flops=flops, bytes_accessed=moved, transcendentals=0
        ),
    )(pick, *operands)


HBM = pl.BlockSpec(memory_space=pltpu.HBM)


def in_hbm(array):
    return pltpu.with_memory_space_constraint(array, pltpu.HBM)


def copy_all(pairs, semaphores):
    copies = [
        pltpu.make_async_copy(source, target, semaphores.at[i])
        for i, (source, target) in enumerate(pairs)
    ]
    for copy in copies:
        copy.start()
    for copy in copies:
        copy.wait()


def product_kernel(fetch, place, pick, grads, weight, *rest):
    rest, scratch = rest[: 1 + (place is not None)], rest[1 + (place is not None) :]
    scratch = list(scratch)
    if fetch:
        held, semaphores = scratch.pop(0), scratch.pop(0)
        copy_all([(grads.at[i, pick[0]], held.at[i]) for i in range(8)], semaphores)
    else:
        held = grads
    product = times_transposed(held[...].reshape(512, held.shape[-1]), weight[...])
    features = product.shape[1]
    out = rest[-1]
    gap = jnp.zeros((512, out.shape[-1] - features), jnp.float32)
    if place is None:
        out[:, :features] = product
        out[:, features:] = gap
        return
    sums, semaphores = scratch
    sums[:, :, :features] = (product + rest[0][:, :features]).reshape(8, 64, features)
    sums[:, :, features:] = gap.reshape(8, 64, -1)
    copy_all([(sums.at[i], out.at[place(i)]) for i in range(8)], semaphores)


def x_yh(chip):
    return (chip % 4, chip // 4)


def in_turn(chip):
    return (chip,)


def token_half(half, grads, weight, *received, fetch=False, place=None):
    tokens, width = grads.shape
    columns = lanes(weight.shape[0])
    grads = grads.reshape(8, 2, 64, width)
    eight = pltpu.SemaphoreType.DMA((8,))
    scratch = [pltpu.VMEM((8, 64, width), grads.dtype), eight] if fetch else []
    if received:
        lead = (4, 2) if place is x_yh else (8,)
        out = pltpu.HBM(lead + (64, columns), jnp.float32)
        scratch += [pltpu.VMEM((8, 64, columns), jnp.float32), eight]
    else:
        out = jax.ShapeDtypeStruct((512, columns), jnp.float32)
    part = pl.BlockSpec((8, 1, 64, width), lambda i, pick: (0, pick[0], 0, 0))
    return call(
        functools.partial(product_kernel, fetch, place),
        [out],
        [HBM if received else None],
        [HBM if fetch else part, None] + [None] * len(received),
        half.reshape(1),
        in_hbm(grads) if fetch else grads,
        weight,
        *received,
        flops=tokens * columns * width,
        scratch=scratch,
    )[0]


def sum_along_x_kernel(pick, parts, near, far, held, semaphores):
    copy_all(
        [(parts.at[i % 4, i // 4], held.at[i // 4, i % 4]) for i in range(8)],
        semaphores,
    )
    first, second = jnp.sum(held[0], axis=0), jnp.sum(held[1], axis=0)
    near[...] = jnp.where(pick[0] == 0, first, second)
    far[...] = jnp.where(pick[0] == 0, second, first)


def sum_along_x(yh, parts):
    columns = parts.shape[-1]
    return call(
        sum_along_x_kernel,
        [jax.ShapeDtypeStruct((64, columns), jnp.float32)] * 2,
        [None] * 2,
        [HBM],
        yh.reshape(1),
        in_hbm(parts),
        scratch=[
            pltpu.VMEM((2, 4, 64, columns), jnp.float32),
            pltpu.SemaphoreType.DMA((8,)),
        ],
    )


def finish_kernel(pick, *refs):
    parts, outs = refs[:4], refs[4:]
    for near, far, out in zip(parts[::2], parts[1::2], outs):
        out[...] = (near[...] + far[...])[:, : out.shape[1]].astype(jnp.bfloat16)


def momentum_kernel(
    first, pick, inputs, inputs_theirs, grads, grads_theirs, moment, step, momentum
):
    rows = pl.ds(first, moment.shape[0])
    tokens = grads.shape[0] * grads.shape[2]
    width = grads.shape[-1]
    gradient = rows_product(
        inputs[..., rows].reshape(tokens, -1), grads[...].reshape(tokens, width)
    ) + rows_product(
        inputs_theirs[..., rows].reshape(tokens, -1),
        grads_theirs[...].reshape(tokens, width),
    )
    gradient = gradient * (1.0 / math.sqrt(float(2 * tokens)))
    held = moment[...].astype(jnp.float32)
    blended = 0.9 * held + 0.1 * gradient
    step[...] = (blended / jnp.sqrt(blended * blended + 0.01)).astype(jnp.bfloat16)
    momentum[...] = (0.99 * held + 0.01 * gradient).astype(jnp.bfloat16)


def momentum_step(core, inputs, inputs_theirs, first, grads, moment):
    tokens, width = grads.shape
    grads = grads.reshape(tokens // 128, 2, 64, width)
    block = (tokens // 128, 1, 64, width)
    return call(
        functools.partial(momentum_kernel, first),
        [jax.ShapeDtypeStruct(moment.shape, jnp.bfloat16)] * 2,
        [None] * 2,
        [
            None,
            None,
            pl.BlockSpec(block, lambda i, pick: (0, pick[0], 0, 0)),
            pl.BlockSpec(block, lambda i, pick: (0, 1 - pick[0], 0, 0)),
            None,
        ],
        core.reshape(1),
        inputs,
        inputs_theirs,
        grads,
        grads,
        moment,
        flops=2 * tokens * moment.size,
    )


def on_device(
    block_input,
    context,
    query_grad,
    output_grad,
    query_weight,
    query_moment,
    output_weight,
    output_moment,
):
    core, yh = lax.axis_index("core"), lax.axis_index("yh")
    width = query_grad.shape[1]
    grads = side_by_side(query_grad, output_grad)
    grads = lax.all_gather(grads, "yl", axis=0, tiled=True)
    output_part, block_input, context = lax.optimization_barrier(
        (grads[:, PAD:], block_input, context)
    )
    output_all = lax.all_gather(output_part, "z", axis=0, tiled=True)
    inputs = side_by_side(block_input, context)
    inputs = jnp.broadcast_to(inputs[None], (8,) + inputs.shape)
    inputs = lax.all_to_all(inputs, ("yh", "x"), 0, 0, tiled=True)
    query_all = lax.all_gather(grads[:, :width], "z", axis=0, tiled=True)
    query_all, inputs = lax.optimization_barrier((query_all, inputs))
    query_theirs = token_half(1 - core, query_all, query_weight)
    query_theirs = lax.ppermute(query_theirs, "core", SWAP)
    inputs_theirs = lax.ppermute(inputs, "core", SWAP)
    query_pair = token_half(core, query_all, query_weight, query_theirs, place=x_yh)
    query_pair, inputs_theirs = lax.optimization_barrier((query_pair, inputs_theirs))
    query_parts = lax.all_to_all(query_pair, "x", 0, 0, tiled=True)
    output_theirs = token_half(1 - core, output_all, output_weight, fetch=True)
    output_theirs = lax.ppermute(output_theirs, "core", SWAP)
    output_pair = token_half(
        core, output_all, output_weight, output_theirs, fetch=True, place=x_yh
    )
    query_step, query_momentum = momentum_step(
        core, inputs, inputs_theirs, 0, query_all, query_moment
    )
    output_step, output_momentum = momentum_step(
        core, inputs, inputs_theirs, PAD, output_all, output_moment
    )
    query_parts, output_pair, query_step, output_step = lax.optimization_barrier(
        (query_parts, output_pair, query_step, output_step)
    )
    output_parts = lax.all_to_all(output_pair, "x", 0, 0, tiled=True)
    query_near, query_far = sum_along_x(yh, query_parts)
    query_far = lax.ppermute(query_far, "yh", SWAP)
    output_near, output_far = sum_along_x(yh, output_parts)
    output_far = lax.ppermute(output_far, "yh", SWAP)
    input_grad, context_grad = call(
        finish_kernel,
        [
            jax.ShapeDtypeStruct(block_input.shape, jnp.bfloat16),
            jax.ShapeDtypeStruct(context.shape, jnp.bfloat16),
        ],
        [None] * 2,
        [None] * 4,
        jnp.zeros((1,), jnp.int32),
        query_near,
        query_far,
        output_near,
        output_far,
    )
    return (
        input_grad,
        context_grad,
        query_step,
        query_momentum,
        output_step,
        output_momentum,
    )


def solution(mesh):
    split = Mesh(mesh.devices.reshape(2, 4, 2, 8, 4), GX + GYZ)
    rows, columns = P(GX, GYZ), P(GYZ, GX)
    return jax.shard_map(
        on_device,
        mesh=split,
        in_specs=(rows, rows) + (columns,) * 6,
        out_specs=(rows, rows) + (columns,) * 4,
        check_vma=False,
    )
```

time: 135 us -> 133 us (0.985)
  the two profiles are of different devices: /device:TPU:16 before, /device:TPU:4 now
where the time goes in v3:
time: 133 us; the launch traced here: 132 us
  blocking collectives  50.7 us (38%)
  starting transfers between devices  40.1 us (30%)
  between operations  14.2 us (11%)
  Pallas kernels  13.9 us (10%)
  waiting for transfers between devices  7.79 us (6%)
  local copies, waits for them, and re-layouts  4.55 us (3%)
    all_gather x1, blocking collectives, on_device(): query_all = lax.all_gather(grads[:, :width], 'z', axis=0, tiled=True)  35.9 us
    all_gather x1, blocking collectives, on_device(): grads = lax.all_gather(grads, 'yl', axis=0, tiled=True)  14.8 us
    pallas_call x9, Pallas kernels, call(): pl.pallas_call(kernel, grid_spec=pltpu.PrefetchScalarGridSpec(num_scalar_...  13.9 us
    all_to_all x1, starting transfers between devices, on_device(): inputs = lax.all_to_all(inputs, ('yh', 'x'), 0, 0, tiled=True)  10.2 us
    ppermute x1, starting transfers between devices, on_device(): query_far = lax.ppermute(query_far, 'yh', SWAP)  7.42 us
    all_to_all x1, starting transfers between devices, on_device(): output_parts = lax.all_to_all(output_pair, 'x', 0, 0, tiled=True)  6.41 us
    ppermute x1, waiting for transfers between devices, on_device(): output_far = lax.ppermute(output_far, 'yh', SWAP)  5.92 us
    ppermute x1, starting transfers between devices, on_device(): output_far = lax.ppermute(output_far, 'yh', SWAP)  4.83 us
  transfers between devices with their start and end apart: 9, of which 3 were waited for; matrix products, arithmetic and copies ran while one was open for 1% of the time, Pallas kernels for 10%

profile of v3, /device:TPU:4, one launch (start us, length us, event | category | flops | bytes accessed | tf_op | source)
XLA Modules:
  0.0 132.2 jit_solution(6894976964781311362)
XLA Ops:
  7.2 0.9 concatenate.6
  8.2 14.8 %all_gather.9 = bf16[128,1440]{1,0:T(8,128)(2,1)S(1)} all-gather(bf16[32,1440]{1,0:T(8,128)(2,1)S(1)} %concatenate.6), channel_id=1, replica_groups=mesh['yh'=2,'x'=4,'core'=2,'z'=8,'yl'=4] {'yl'}, dimensions={0}, use_global_device_ids=true | all-gather | bytes 460800 | tf_op jit(solution)/shard_map/all_gather | solution.py:224
  23.8 0.9 pad_maximum_fusion
  24.7 0.9 broadcast_in_dim.14
  25.7 10.2 %all-to-all-start = ((bf16[8,64,744]{2,1,0:T(8,128)(2,1)}), bf16[8,64,744]{2,1,0:T(8,128)(2,1)S(1)}, u32[]{:S(2)}, u32[]{:S(2)}) async-start(bf16[8,64,744]{2,1,0:T(8,128)(2,1)} %broadcast_in_dim.14), calls=%async_computation | async-start | bytes 1572864 | tf_op jit(solution)/shard_map/all_to_all | solution.py:231
  35.9 35.9 %all_gather.10 = bf16[1024,464]{1,0:T(8,128)(2,1)S(1)} all-gather(bf16[128,464]{1,0:T(8,128)(2,1)S(1)} %slice.8), channel_id=1, replica_groups=mesh['yh'=2,'x'=4,'core'=2,'z'=8,'yl'=4] {'z'}, dimensions={0}, use_global_device_ids=true | all-gather | bytes 1069056 | tf_op jit(solution)/shard_map/all_gather | solution.py:232
  72.3 1.9 %collective-permute-start = (f32[512,512]{1,0:T(8,128)S(1)}, f32[512,512]{1,0:T(8,128)S(1)}, u32[]{:S(2)}, u32[]{:S(2)}) collective-permute-start(f32[512,512]{1,0:T(8,128)S(1)} %shard_map.127), channel_id=1, source_target_pairs={{0,32},{32,0},{1,33},{33,1},{2,34},{34,2},{3,35},{35,3},{4,36},{36... | collective-permute-start | bytes 3145736 | tf_op jit(solution)/shard_map/ppermute | solution.py:235
  74.2 2.4 %collective-permute-start.1 = (bf16[8,64,744]{2,1,0:T(8,128)(2,1)S(1)}, bf16[8,64,744]{2,1,0:T(8,128)(2,1)S(1)}, u32[]{:S(2)}, u32[]{:S(2)}) collective-permute-start(bf16[8,64,744]{2,1,0:T(8,128)(2,1)S(1)} %all-to-all-done.inputs), channel_id=1, source_target_pairs={{0,32},{32,0},{1,33},{33,1},{2,34},{34,2},{3,35},{35,3},{4,36},{36... | collective-permute-start | bytes 2285576 | tf_op jit(solution)/shard_map/ppermute | solution.py:236
  76.9 1.0 copy-done.3
  77.9 1.5 %shard_map.128 = f32[4,2,64,512]{3,2,1,0:T(8,128)} custom-call(s32[1]{0:T(128)} %bitcast.1.pick, bf16[8,2,64,464]{3,2,1,0:T(8,128)(2,1)S(1)} %bitcast.10, bf16[464,464]{1,0:T(8,128)(2,1)S(1)} %copy-done.3, f32[512,512]{1,0:T(8,128)S(1)} %collective-permute-done.rest_0_), custom_call_target="tpu_custom_call" | custom-call | flops 243269632 | bytes 2429440 | tf_op jit(solution)/shard_map/pallas_call | solution.py:43
  79.4 4.8 %all-to-all-start.1 = ((f32[4,2,64,512]{3,2,1,0:T(8,128)}), f32[4,2,64,512]{3,2,1,0:T(8,128)}, u32[]{:S(2)}, u32[]{:S(2)}) async-start(f32[4,2,64,512]{3,2,1,0:T(8,128)} %shard_map.128), calls=%async_computation.1 | async-start | bytes 2097152 | tf_op jit(solution)/shard_map/all_to_all | solution.py:239
  84.2 1.9 %shard_map.129 = f32[512,256]{1,0:T(8,128)S(1)} custom-call(s32[1]{0:T(128)} %bitcast.3.pick, bf16[8,2,64,928]{3,2,1,0:T(8,128)(2,1)} %bitcast.5, bf16[232,928]{1,0:T(8,128)(2,1)S(1)} %copy-done.1), custom_call_target="tpu_custom_call" | custom-call | flops 243269632 | bytes 2331136 | tf_op jit(solution)/shard_map/pallas_call | solution.py:43
  86.1 2.1 %collective-permute-start.2 = (f32[512,256]{1,0:T(8,128)S(1)}, f32[512,256]{1,0:T(8,128)S(1)}, u32[]{:S(2)}, u32[]{:S(2)}) collective-permute-start(f32[512,256]{1,0:T(8,128)S(1)} %shard_map.129), channel_id=1, source_target_pairs={{0,32},{32,0},{1,33},{33,1},{2,34},{34,2},{3,35},{35,3},{4,36},{36... | collective-permute-start | bytes 1572872 | tf_op jit(solution)/shard_map/ppermute | solution.py:241
  88.2 2.1 %shard_map.131 = (bf16[464,464]{1,0:T(8,128)(2,1)}, bf16[464,464]{1,0:T(8,128)(2,1)}) custom-call(s32[1]{0:T(128)} %bitcast.1.pick, bf16[8,64,744]{2,1,0:T(8,128)(2,1)S(1)} %all-to-all-done.inputs, bf16[8,64,744]{2,1,0:T(8,128)(2,1)S(1)} %collective-permute-done.1.inputs_theirs, bf16[8,2,64,464]{3,2,1,0:T(8,128)(2,1)S(1)} %bitcast.11, ...), custom_call_target="tpu_custom_call" | custom-call | flops 440926208 | bytes 3854848 | tf_op jit(solution)/shard_map/pallas_call | solution.py:43
  90.3 2.1 %shard_map.132 = (bf16[232,928]{1,0:T(8,128)(2,1)}, bf16[232,928]{1,0:T(8,128)(2,1)}) custom-call(s32[1]{0:T(128)} %bitcast.1.pick, bf16[8,64,744]{2,1,0:T(8,128)(2,1)S(1)} %all-to-all-done.inputs, bf16[8,64,744]{2,1,0:T(8,128)(2,1)S(1)} %collective-permute-done.1.inputs_theirs, bf16[8,2,64,928]{3,2,1,0:T(8,128)(2,1)S(1)} %bitcast.7, ...), custom_call_target="tpu_custom_call" | custom-call | flops 440926208 | bytes 5755392 | tf_op jit(solution)/shard_map/pallas_call | solution.py:43
  92.4 2.7 %shard_map.130 = f32[4,2,64,256]{3,2,1,0:T(8,128)} custom-call(s32[1]{0:T(128)} %bitcast.1.pick, bf16[8,2,64,928]{3,2,1,0:T(8,128)(2,1)} %bitcast.6, bf16[232,928]{1,0:T(8,128)(2,1)S(1)} %copy-done.1, f32[512,256]{1,0:T(8,128)S(1)} %collective-permute-done.2.rest_0_), custom_call_target="tpu_custom_call" | custom-call | flops 243269632 | bytes 2855424 | tf_op jit(solution)/shard_map/pallas_call | solution.py:43
  95.1 1.6 %all-to-all-done.1.parts = f32[4,2,64,512]{3,2,1,0:T(8,128)} async-done(((f32[4,2,64,512]{3,2,1,0:T(8,128)}), f32[4,2,64,512]{3,2,1,0:T(8,128)}, u32[]{:S(2)}, u32[]{:S(2)}) %all-to-all-start.1) | async-done | bytes 1048608 | tf_op jit(solution)/shard_map/all_to_all | solution.py:239
  96.7 6.4 %all-to-all-start.2 = ((f32[4,2,64,256]{3,2,1,0:T(8,128)}), f32[4,2,64,256]{3,2,1,0:T(8,128)S(1)}, u32[]{:S(2)}, u32[]{:S(2)}) async-start(f32[4,2,64,256]{3,2,1,0:T(8,128)} %shard_map.130), calls=%async_computation.2 | async-start | bytes 1048576 | tf_op jit(solution)/shard_map/all_to_all | solution.py:254
  103.2 1.4 %shard_map.133 = (f32[64,512]{1,0:T(8,128)S(1)}, f32[64,512]{1,0:T(8,128)S(1)}) custom-call(s32[1]{0:T(128)} %bitcast.pick, f32[4,2,64,512]{3,2,1,0:T(8,128)} %all-to-all-done.1.parts), custom_call_target="tpu_custom_call" | custom-call | bytes 1048576 | tf_op jit(solution)/shard_map/pallas_call | solution.py:43
  104.6 7.4 %collective-permute-start.3 = (f32[64,512]{1,0:T(8,128)S(1)}, f32[64,512]{1,0:T(8,128)S(1)}, u32[]{:S(2)}, u32[]{:S(2)}) collective-permute-start(f32[64,512]{1,0:T(8,128)S(1)} %get-tuple-element.38), channel_id=1, source_target_pairs={{0,256},{256,0},{1,257},{257,1},{2,258},{258,2},{3,259},{259,3},{4... | collective-permute-start | bytes 393224 | tf_op jit(solution)/shard_map/ppermute | solution.py:256
  112.0 0.8 copy-done.6
  112.8 1.2 shard_map.134
  114.0 4.8 %collective-permute-start.4 = (f32[64,256]{1,0:T(8,128)S(1)}, f32[64,256]{1,0:T(8,128)S(1)}, u32[]{:S(2)}, u32[]{:S(2)}) collective-permute-start(f32[64,256]{1,0:T(8,128)S(1)} %get-tuple-element.41), channel_id=1, source_target_pairs={{0,256},{256,0},{1,257},{257,1},{2,258},{258,2},{3,259},{259,3},{4... | collective-permute-start | bytes 196616 | tf_op jit(solution)/shard_map/ppermute | solution.py:258
  118.8 5.9 %collective-permute-done.4.refs_3_ = f32[64,256]{1,0:T(8,128)S(1)} collective-permute-done((f32[64,256]{1,0:T(8,128)S(1)}, f32[64,256]{1,0:T(8,128)S(1)}, u32[]{:S(2)}, u32[]{:S(2)}) %collective-permute-start.4) | collective-permute-done | bytes 65568 | tf_op jit(solution)/shard_map/ppermute | solution.py:258
  (28 shorter events, 2.2 us)
Async XLA Ops:
  7.2 77.1 %all-gather.2.cloned.1.call-start = ((), (), s32[]{:S(2)}) async-start(), calls=%async_computation.3 | async-start | bytes 2359296 | tf_op jit(solution)/shard_map/all_gather | solution.py:228
  23.7 48.1 %copy-start.2 = (bf16[464,464]{1,0:T(8,128)(2,1)S(1)}, bf16[464,464]{1,0:T(8,128)(2,1)}, u32[]{:S(2)}) copy-start(bf16[464,464]{1,0:T(8,128)(2,1)} %weight.5) | copy-start | bytes 1291780
  25.7 46.2 %all-to-all-start = ((bf16[8,64,744]{2,1,0:T(8,128)(2,1)}), bf16[8,64,744]{2,1,0:T(8,128)(2,1)S(1)}, u32[]{:S(2)}, u32[]{:S(2)}) async-start(bf16[8,64,744]{2,1,0:T(8,128)(2,1)} %broadcast_in_dim.14), calls=%async_computation | async-start | bytes 1572864 | tf_op jit(solution)/shard_map/all_to_all | solution.py:231
  72.3 4.6 %collective-permute-start = (f32[512,512]{1,0:T(8,128)S(1)}, f32[512,512]{1,0:T(8,128)S(1)}, u32[]{:S(2)}, u32[]{:S(2)}) collective-permute-start(f32[512,512]{1,0:T(8,128)S(1)} %shard_map.127), channel_id=1, source_target_pairs={{0,32},{32,0},{1,33},{33,1},{2,34},{34,2},{3,35},{35,3},{4,36},{36... | collective-permute-start | bytes 3145736 | tf_op jit(solution)/shard_map/ppermute | solution.py:235
  74.2 5.2 %collective-permute-start.1 = (bf16[8,64,744]{2,1,0:T(8,128)(2,1)S(1)}, bf16[8,64,744]{2,1,0:T(8,128)(2,1)S(1)}, u32[]{:S(2)}, u32[]{:S(2)}) collective-permute-start(bf16[8,64,744]{2,1,0:T(8,128)(2,1)S(1)} %all-to-all-done.inputs), channel_id=1, source_target_pairs={{0,32},{32,0},{1,33},{33,1},{2,34},{34,2},{3,35},{35,3},{4,36},{36... | collective-permute-start | bytes 2285576 | tf_op jit(solution)/shard_map/ppermute | solution.py:236
  76.9 1.0 copy-start.3
  77.9 6.3 %copy-start.1 = (bf16[232,928]{1,0:T(8,128)(2,1)S(1)}, bf16[232,928]{1,0:T(8,128)(2,1)}, u32[]{:S(2)}) copy-start(bf16[232,928]{1,0:T(8,128)(2,1)} %weight.7) | copy-start | bytes 1291780
  79.4 17.3 %all-to-all-start.1 = ((f32[4,2,64,512]{3,2,1,0:T(8,128)}), f32[4,2,64,512]{3,2,1,0:T(8,128)}, u32[]{:S(2)}, u32[]{:S(2)}) async-start(f32[4,2,64,512]{3,2,1,0:T(8,128)} %shard_map.128), calls=%async_computation.1 | async-start | bytes 2097152 | tf_op jit(solution)/shard_map/all_to_all | solution.py:239
  84.2 4.0 %copy-start.4 = (bf16[464,464]{1,0:T(8,128)(2,1)S(1)}, bf16[464,464]{1,0:T(8,128)(2,1)}, u32[]{:S(2)}) copy-start(bf16[464,464]{1,0:T(8,128)(2,1)} %moment.2) | copy-start | bytes 1291780
  86.1 4.2 %copy-start = (bf16[1024,928]{1,0:T(8,128)(2,1)S(1)}, bf16[1024,928]{1,0:T(8,128)(2,1)}, u32[]{:S(2)}) copy-start(bf16[1024,928]{1,0:T(8,128)(2,1)} %all-gather.2.cloned.1.call-done) | copy-start | bytes 5701636
  86.1 4.2 %copy-start.5 = (bf16[232,928]{1,0:T(8,128)(2,1)S(1)}, bf16[232,928]{1,0:T(8,128)(2,1)}, u32[]{:S(2)}) copy-start(bf16[232,928]{1,0:T(8,128)(2,1)} %moment.3) | copy-start | bytes 1291780
  86.1 6.3 %collective-permute-start.2 = (f32[512,256]{1,0:T(8,128)S(1)}, f32[512,256]{1,0:T(8,128)S(1)}, u32[]{:S(2)}, u32[]{:S(2)}) collective-permute-start(f32[512,256]{1,0:T(8,128)S(1)} %shard_map.129), channel_id=1, source_target_pairs={{0,32},{32,0},{1,33},{33,1},{2,34},{34,2},{3,35},{35,3},{4,36},{36... | collective-permute-start | bytes 1572872 | tf_op jit(solution)/shard_map/ppermute | solution.py:241
  96.7 15.2 %all-to-all-start.2 = ((f32[4,2,64,256]{3,2,1,0:T(8,128)}), f32[4,2,64,256]{3,2,1,0:T(8,128)S(1)}, u32[]{:S(2)}, u32[]{:S(2)}) async-start(f32[4,2,64,256]{3,2,1,0:T(8,128)} %shard_map.130), calls=%async_computation.2 | async-start | bytes 1048576 | tf_op jit(solution)/shard_map/all_to_all | solution.py:254
  104.6 14.3 %collective-permute-start.3 = (f32[64,512]{1,0:T(8,128)S(1)}, f32[64,512]{1,0:T(8,128)S(1)}, u32[]{:S(2)}, u32[]{:S(2)}) collective-permute-start(f32[64,512]{1,0:T(8,128)S(1)} %get-tuple-element.38), channel_id=1, source_target_pairs={{0,256},{256,0},{1,257},{257,1},{2,258},{258,2},{3,259},{259,3},{4... | collective-permute-start | bytes 393224 | tf_op jit(solution)/shard_map/ppermute | solution.py:256
  112.0 0.8 copy-start.6
  114.0 10.8 %collective-permute-start.4 = (f32[64,256]{1,0:T(8,128)S(1)}, f32[64,256]{1,0:T(8,128)S(1)}, u32[]{:S(2)}, u32[]{:S(2)}) collective-permute-start(f32[64,256]{1,0:T(8,128)S(1)} %get-tuple-element.41), channel_id=1, source_target_pairs={{0,256},{256,0},{1,257},{257,1},{2,258},{258,2},{3,259},{259,3},{4... | collective-permute-start | bytes 196616 | tf_op jit(solution)/shard_map/ppermute | solution.py:258
Sparse Core Ops, SparseCore 0:
  23.8 53.5 all-gather.1

commit v4 on v3

--- a/solution.py
+++ b/solution.py
@@ -233,29 +233,30 @@
     query_all, inputs = lax.optimization_barrier((query_all, inputs))
     query_theirs = token_half(1 - core, query_all, query_weight)
     query_theirs = lax.ppermute(query_theirs, "core", SWAP)
-    inputs_theirs = lax.ppermute(inputs, "core", SWAP)
     query_pair = token_half(core, query_all, query_weight, query_theirs, place=x_yh)
-    query_pair, inputs_theirs = lax.optimization_barrier((query_pair, inputs_theirs))
+    query_pair, inputs = lax.optimization_barrier((query_pair, inputs))
     query_parts = lax.all_to_all(query_pair, "x", 0, 0, tiled=True)
     output_theirs = token_half(1 - core, output_all, output_weight, fetch=True)
     output_theirs = lax.ppermute(output_theirs, "core", SWAP)
+    inputs_theirs = lax.ppermute(inputs, "core", SWAP)
     output_pair = token_half(
         core, output_all, output_weight, output_theirs, fetch=True, place=x_yh
     )
     query_step, query_momentum = momentum_step(
         core, inputs, inputs_theirs, 0, query_all, query_moment
     )
-    output_step, output_momentum = momentum_step(
-        core, inputs, inputs_theirs, PAD, output_all, output_moment
-    )
-    query_parts, output_pair, query_step, output_step = lax.optimization_barrier(
-        (query_parts, output_pair, query_step, output_step)
+    query_parts, output_pair, query_step = lax.optimization_barrier(
+        (query_parts, output_pair, query_step)
     )
     output_parts = lax.all_to_all(output_pair, "x", 0, 0, tiled=True)
     query_near, query_far = sum_along_x(yh, query_parts)
     query_far = lax.ppermute(query_far, "yh", SWAP)
     output_near, output_far = sum_along_x(yh, output_parts)
     output_far = lax.ppermute(output_far, "yh", SWAP)
+    output_step, output_momentum = momentum_step(
+        core, inputs, inputs_theirs, PAD, output_all, output_moment
+    )
+    output_far, output_step = lax.optimization_barrier((output_far, output_step))
     input_grad, context_grad = call(
         finish_kernel,
         [

time: 133 us -> 135 us (1.015)
  Pallas kernels: 13.9 us -> 15.5 us
    ppermute x1, waiting for transfers between devices: 5.92 us -> 2.3 us  [on_device(): output_far = lax.ppermute(output_far, 'yh', SWAP)]
    ppermute x1, waiting for transfers between devices: 0.21 us -> 2.63 us  [on_device(): query_theirs = lax.ppermute(query_theirs, 'core', SWAP)]
    all_to_all x1, waiting for transfers between devices: 1.63 us -> 4.04 us  [on_device(): query_parts = lax.all_to_all(query_pair, 'x', 0, 0, tiled=True)]
    pallas_call x9, Pallas kernels: 13.9 us -> 15.5 us  [call(): pl.pallas_call(kernel, grid_spec=pltpu.PrefetchScalarGridSpec(num_scalar_...]
where the time goes in v4:
time: 135 us; the launch traced here: 134 us
  blocking collectives  50.7 us (38%)
  starting transfers between devices  39.8 us (29%)
  Pallas kernels  15.5 us (11%)
  between operations  14.2 us (11%)
  waiting for transfers between devices  9 us (7%)
  local copies, waits for them, and re-layouts  3.86 us (3%)
    all_gather x1, blocking collectives, on_device(): query_all = lax.all_gather(grads[:, :width], 'z', axis=0, tiled=True)  35.9 us
    pallas_call x9, Pallas kernels, call(): pl.pallas_call(kernel, grid_spec=pltpu.PrefetchScalarGridSpec(num_scalar_...  15.5 us
    all_gather x1, blocking collectives, on_device(): grads = lax.all_gather(grads, 'yl', axis=0, tiled=True)  14.8 us
    all_to_all x1, starting transfers between devices, on_device(): inputs = lax.all_to_all(inputs, ('yh', 'x'), 0, 0, tiled=True)  10.2 us
    ppermute x1, starting transfers between devices, on_device(): query_far = lax.ppermute(query_far, 'yh', SWAP)  7.22 us
    all_to_all x1, starting transfers between devices, on_device(): output_parts = lax.all_to_all(output_pair, 'x', 0, 0, tiled=True)  7.05 us
    all_to_all x1, starting transfers between devices, on_device(): query_parts = lax.all_to_all(query_pair, 'x', 0, 0, tiled=True)  4.82 us
    ppermute x1, starting transfers between devices, on_device(): output_far = lax.ppermute(output_far, 'yh', SWAP)  4.55 us
  transfers between devices with their start and end apart: 9, of which 3 were waited for; matrix products, arithmetic and copies ran while one was open for 1% of the time, Pallas kernels for 10%

profile of v4, /device:TPU:4, one launch (start us, length us, event | category | flops | bytes accessed | tf_op | source)
XLA Modules:
  0.0 134.0 jit_solution(15802904066099362401)
XLA Ops:
  7.2 0.9 concatenate.6
  8.2 14.8 %all_gather.9 = bf16[128,1440]{1,0:T(8,128)(2,1)S(1)} all-gather(bf16[32,1440]{1,0:T(8,128)(2,1)S(1)} %concatenate.6), channel_id=1, replica_groups=mesh['yh'=2,'x'=4,'core'=2,'z'=8,'yl'=4] {'yl'}, dimensions={0}, use_global_device_ids=true | all-gather | bytes 460800 | tf_op jit(solution)/shard_map/all_gather | solution.py:224
  24.7 0.9 broadcast_in_dim.14
  25.7 10.2 %all-to-all-start = ((bf16[8,64,744]{2,1,0:T(8,128)(2,1)}), bf16[8,64,744]{2,1,0:T(8,128)(2,1)S(1)}, u32[]{:S(2)}, u32[]{:S(2)}) async-start(bf16[8,64,744]{2,1,0:T(8,128)(2,1)} %broadcast_in_dim.14), calls=%async_computation | async-start | bytes 1572864 | tf_op jit(solution)/shard_map/all_to_all | solution.py:231
  35.9 35.9 %all_gather.10 = bf16[1024,464]{1,0:T(8,128)(2,1)S(1)} all-gather(bf16[128,464]{1,0:T(8,128)(2,1)S(1)} %slice.8), channel_id=1, replica_groups=mesh['yh'=2,'x'=4,'core'=2,'z'=8,'yl'=4] {'z'}, dimensions={0}, use_global_device_ids=true | all-gather | bytes 1069056 | tf_op jit(solution)/shard_map/all_gather | solution.py:232
  72.3 1.9 %collective-permute-start = (f32[512,512]{1,0:T(8,128)S(1)}, f32[512,512]{1,0:T(8,128)S(1)}, u32[]{:S(2)}, u32[]{:S(2)}) collective-permute-start(f32[512,512]{1,0:T(8,128)S(1)} %shard_map.127), channel_id=1, source_target_pairs={{0,32},{32,0},{1,33},{33,1},{2,34},{34,2},{3,35},{35,3},{4,36},{36... | collective-permute-start | bytes 3145736 | tf_op jit(solution)/shard_map/ppermute | solution.py:235
  74.2 2.6 %collective-permute-done.rest_0_ = f32[512,512]{1,0:T(8,128)S(1)} collective-permute-done((f32[512,512]{1,0:T(8,128)S(1)}, f32[512,512]{1,0:T(8,128)S(1)}, u32[]{:S(2)}, u32[]{:S(2)}) %collective-permute-start) | collective-permute-done | bytes 1048608 | tf_op jit(solution)/shard_map/ppermute | solution.py:235
  76.9 1.5 %shard_map.128 = f32[4,2,64,512]{3,2,1,0:T(8,128)} custom-call(s32[1]{0:T(128)} %bitcast.1.pick, bf16[8,2,64,464]{3,2,1,0:T(8,128)(2,1)S(1)} %bitcast.10, bf16[464,464]{1,0:T(8,128)(2,1)S(1)} %copy-done.4, f32[512,512]{1,0:T(8,128)S(1)} %collective-permute-done.rest_0_), custom_call_target="tpu_custom_call" | custom-call | flops 243269632 | bytes 2429440 | tf_op jit(solution)/shard_map/pallas_call | solution.py:43
  78.4 2.0 %collective-permute-start.2 = (bf16[8,64,744]{2,1,0:T(8,128)(2,1)S(1)}, bf16[8,64,744]{2,1,0:T(8,128)(2,1)S(1)}, u32[]{:S(2)}, u32[]{:S(2)}) collective-permute-start(bf16[8,64,744]{2,1,0:T(8,128)(2,1)S(1)} %all-to-all-done.inputs), channel_id=1, source_target_pairs={{0,32},{32,0},{1,33},{33,1},{2,34},{34,2},{3,35},{35,3},{4,36},{36... | collective-permute-start | bytes 2285576 | tf_op jit(solution)/shard_map/ppermute | solution.py:241
  80.4 4.8 %all-to-all-start.1 = ((f32[4,2,64,512]{3,2,1,0:T(8,128)}), f32[4,2,64,512]{3,2,1,0:T(8,128)}, u32[]{:S(2)}, u32[]{:S(2)}) async-start(f32[4,2,64,512]{3,2,1,0:T(8,128)} %shard_map.128), calls=%async_computation.1 | async-start | bytes 2097152 | tf_op jit(solution)/shard_map/all_to_all | solution.py:238
  85.3 1.9 %shard_map.129 = f32[512,256]{1,0:T(8,128)S(1)} custom-call(s32[1]{0:T(128)} %bitcast.3.pick, bf16[8,2,64,928]{3,2,1,0:T(8,128)(2,1)} %bitcast.5, bf16[232,928]{1,0:T(8,128)(2,1)S(1)} %copy-done.3), custom_call_target="tpu_custom_call" | custom-call | flops 243269632 | bytes 2331136 | tf_op jit(solution)/shard_map/pallas_call | solution.py:43
  87.1 1.9 %collective-permute-start.1 = (f32[512,256]{1,0:T(8,128)S(1)}, f32[512,256]{1,0:T(8,128)S(1)}, u32[]{:S(2)}, u32[]{:S(2)}) collective-permute-start(f32[512,256]{1,0:T(8,128)S(1)} %shard_map.129), channel_id=1, source_target_pairs={{0,32},{32,0},{1,33},{33,1},{2,34},{34,2},{3,35},{35,3},{4,36},{36... | collective-permute-start | bytes 1572872 | tf_op jit(solution)/shard_map/ppermute | solution.py:240
  89.1 2.1 %shard_map.131 = (bf16[464,464]{1,0:T(8,128)(2,1)}, bf16[464,464]{1,0:T(8,128)(2,1)}) custom-call(s32[1]{0:T(128)} %bitcast.1.pick, bf16[8,64,744]{2,1,0:T(8,128)(2,1)S(1)} %all-to-all-done.inputs, bf16[8,64,744]{2,1,0:T(8,128)(2,1)S(1)} %collective-permute-done.2.inputs_theirs, bf16[8,2,64,464]{3,2,1,0:T(8,128)(2,1)S(1)} %bitcast.11, ...), custom_call_target="tpu_custom_call" | custom-call | flops 440926208 | bytes 3854848 | tf_op jit(solution)/shard_map/pallas_call | solution.py:43
  91.2 2.7 %shard_map.130 = f32[4,2,64,256]{3,2,1,0:T(8,128)} custom-call(s32[1]{0:T(128)} %bitcast.1.pick, bf16[8,2,64,928]{3,2,1,0:T(8,128)(2,1)} %bitcast.6, bf16[232,928]{1,0:T(8,128)(2,1)S(1)} %copy-done.3, f32[512,256]{1,0:T(8,128)S(1)} %collective-permute-done.1.rest_0_), custom_call_target="tpu_custom_call" | custom-call | flops 243269632 | bytes 2855424 | tf_op jit(solution)/shard_map/pallas_call | solution.py:43
  94.0 4.0 %all-to-all-done.1.parts = f32[4,2,64,512]{3,2,1,0:T(8,128)} async-done(((f32[4,2,64,512]{3,2,1,0:T(8,128)}), f32[4,2,64,512]{3,2,1,0:T(8,128)}, u32[]{:S(2)}, u32[]{:S(2)}) %all-to-all-start.1) | async-done | bytes 1048608 | tf_op jit(solution)/shard_map/all_to_all | solution.py:238
  98.0 7.1 %all-to-all-start.2 = ((f32[4,2,64,256]{3,2,1,0:T(8,128)}), f32[4,2,64,256]{3,2,1,0:T(8,128)}, u32[]{:S(2)}, u32[]{:S(2)}) async-start(f32[4,2,64,256]{3,2,1,0:T(8,128)} %shard_map.130), calls=%async_computation.2 | async-start | bytes 1048576 | tf_op jit(solution)/shard_map/all_to_all | solution.py:251
  105.1 2.0 %shard_map.132 = (f32[64,512]{1,0:T(8,128)S(1)}, f32[64,512]{1,0:T(8,128)}) custom-call(s32[1]{0:T(128)} %bitcast.pick, f32[4,2,64,512]{3,2,1,0:T(8,128)} %all-to-all-done.1.parts), custom_call_target="tpu_custom_call" | custom-call | bytes 1048576 | tf_op jit(solution)/shard_map/pallas_call | solution.py:43
  107.1 7.2 %collective-permute-start.3 = (f32[64,512]{1,0:T(8,128)}, f32[64,512]{1,0:T(8,128)}, u32[]{:S(2)}, u32[]{:S(2)}) collective-permute-start(f32[64,512]{1,0:T(8,128)} %get-tuple-element.38), channel_id=1, source_target_pairs={{0,256},{256,0},{1,257},{257,1},{2,258},{258,2},{3,259},{259,3},{4... | collective-permute-start | bytes 393224 | tf_op jit(solution)/shard_map/ppermute | solution.py:253
  114.4 1.2 shard_map.133
  115.5 4.5 %collective-permute-start.4 = (f32[64,256]{1,0:T(8,128)S(1)}, f32[64,256]{1,0:T(8,128)S(1)}, u32[]{:S(2)}, u32[]{:S(2)}) collective-permute-start(f32[64,256]{1,0:T(8,128)S(1)} %get-tuple-element.41), channel_id=1, source_target_pairs={{0,256},{256,0},{1,257},{257,1},{2,258},{258,2},{3,259},{259,3},{4... | collective-permute-start | bytes 196616 | tf_op jit(solution)/shard_map/ppermute | solution.py:255
  120.1 1.1 copy-done.2
  121.2 2.1 %shard_map.134 = (bf16[232,928]{1,0:T(8,128)(2,1)}, bf16[232,928]{1,0:T(8,128)(2,1)}) custom-call(s32[1]{0:T(128)} %bitcast.1.pick, bf16[8,64,744]{2,1,0:T(8,128)(2,1)S(1)} %all-to-all-done.inputs, bf16[8,64,744]{2,1,0:T(8,128)(2,1)S(1)} %copy-done.2, bf16[8,2,64,928]{3,2,1,0:T(8,128)(2,1)S(1)} %bitcast.7, bf16[8,2,64,928]{3,2,1,0:T(8,128)(2,1)S(1)} %bitcast.8, ...), custom_call_target="tpu_custom_call" | custom-call | flops 440926208 | bytes 5755392 | tf_op jit(solution)/shard_map/pallas_call | solution.py:43
  123.3 2.3 %collective-permute-done.4.refs_3_ = f32[64,256]{1,0:T(8,128)S(1)} collective-permute-done((f32[64,256]{1,0:T(8,128)S(1)}, f32[64,256]{1,0:T(8,128)S(1)}, u32[]{:S(2)}, u32[]{:S(2)}) %collective-permute-start.4) | collective-permute-done | bytes 65568 | tf_op jit(solution)/shard_map/ppermute | solution.py:255
  125.6 1.6 %shard_map.135 = (bf16[64,464]{1,0:T(8,128)(2,1)}, bf16[64,232]{1,0:T(8,128)(2,1)}) custom-call(s32[1]{0:T(128)} %constant.6.clone.1.pick, f32[64,512]{1,0:T(8,128)S(1)} %get-tuple-element.37.refs_0_, f32[64,512]{1,0:T(8,128)} %collective-permute-done.3.refs_1_, f32[64,256]{1,0:T(8,128)S(1)} %get-tuple-element.40.refs_2_, ...), custom_call_target="tpu_custom_call" | custom-call | bytes 393216 | tf_op jit(solution)/shard_map/pallas_call | solution.py:43
  (28 shorter events, 2.3 us)
Async XLA Ops:
  7.2 78.1 %all-gather.2.cloned.1.call-start = ((), (), s32[]{:S(2)}) async-start(), calls=%async_computation.3 | async-start | bytes 2359296 | tf_op jit(solution)/shard_map/all_gather | solution.py:228
  23.7 48.1 %copy-start.4 = (bf16[464,464]{1,0:T(8,128)(2,1)S(1)}, bf16[464,464]{1,0:T(8,128)(2,1)}, u32[]{:S(2)}) copy-start(bf16[464,464]{1,0:T(8,128)(2,1)} %weight.5) | copy-start | bytes 1291780
  25.7 46.2 %all-to-all-start = ((bf16[8,64,744]{2,1,0:T(8,128)(2,1)}), bf16[8,64,744]{2,1,0:T(8,128)(2,1)S(1)}, u32[]{:S(2)}, u32[]{:S(2)}) async-start(bf16[8,64,744]{2,1,0:T(8,128)(2,1)} %broadcast_in_dim.14), calls=%async_computation | async-start | bytes 1572864 | tf_op jit(solution)/shard_map/all_to_all | solution.py:231
  72.3 4.6 %collective-permute-start = (f32[512,512]{1,0:T(8,128)S(1)}, f32[512,512]{1,0:T(8,128)S(1)}, u32[]{:S(2)}, u32[]{:S(2)}) collective-permute-start(f32[512,512]{1,0:T(8,128)S(1)} %shard_map.127), channel_id=1, source_target_pairs={{0,32},{32,0},{1,33},{33,1},{2,34},{34,2},{3,35},{35,3},{4,36},{36... | collective-permute-start | bytes 3145736 | tf_op jit(solution)/shard_map/ppermute | solution.py:235
  76.9 8.4 %copy-start.3 = (bf16[232,928]{1,0:T(8,128)(2,1)S(1)}, bf16[232,928]{1,0:T(8,128)(2,1)}, u32[]{:S(2)}) copy-start(bf16[232,928]{1,0:T(8,128)(2,1)} %weight.7) | copy-start | bytes 1291780
  78.4 10.7 %collective-permute-start.2 = (bf16[8,64,744]{2,1,0:T(8,128)(2,1)S(1)}, bf16[8,64,744]{2,1,0:T(8,128)(2,1)S(1)}, u32[]{:S(2)}, u32[]{:S(2)}) collective-permute-start(bf16[8,64,744]{2,1,0:T(8,128)(2,1)S(1)} %all-to-all-done.inputs), channel_id=1, source_target_pairs={{0,32},{32,0},{1,33},{33,1},{2,34},{34,2},{3,35},{35,3},{4,36},{36... | collective-permute-start | bytes 2285576 | tf_op jit(solution)/shard_map/ppermute | solution.py:241
  80.4 17.6 %all-to-all-start.1 = ((f32[4,2,64,512]{3,2,1,0:T(8,128)}), f32[4,2,64,512]{3,2,1,0:T(8,128)}, u32[]{:S(2)}, u32[]{:S(2)}) async-start(f32[4,2,64,512]{3,2,1,0:T(8,128)} %shard_map.128), calls=%async_computation.1 | async-start | bytes 2097152 | tf_op jit(solution)/shard_map/all_to_all | solution.py:238
  85.3 3.8 %copy-start.5 = (bf16[464,464]{1,0:T(8,128)(2,1)S(1)}, bf16[464,464]{1,0:T(8,128)(2,1)}, u32[]{:S(2)}) copy-start(bf16[464,464]{1,0:T(8,128)(2,1)} %moment.2) | copy-start | bytes 1291780
  87.1 4.1 %collective-permute-start.1 = (f32[512,256]{1,0:T(8,128)S(1)}, f32[512,256]{1,0:T(8,128)S(1)}, u32[]{:S(2)}, u32[]{:S(2)}) collective-permute-start(f32[512,256]{1,0:T(8,128)S(1)} %shard_map.129), channel_id=1, source_target_pairs={{0,32},{32,0},{1,33},{33,1},{2,34},{34,2},{3,35},{35,3},{4,36},{36... | collective-permute-start | bytes 1572872 | tf_op jit(solution)/shard_map/ppermute | solution.py:240
  89.1 2.2 %copy-start.1 = (bf16[8,64,744]{2,1,0:T(8,128)(2,1)}, bf16[8,64,744]{2,1,0:T(8,128)(2,1)S(1)}, u32[]{:S(2)}) copy-start(bf16[8,64,744]{2,1,0:T(8,128)(2,1)S(1)} %collective-permute-done.2.inputs_theirs) | copy-start | bytes 2285572
  93.9 26.1 %copy-start = (bf16[1024,928]{1,0:T(8,128)(2,1)S(1)}, bf16[1024,928]{1,0:T(8,128)(2,1)}, u32[]{:S(2)}) copy-start(bf16[1024,928]{1,0:T(8,128)(2,1)} %all-gather.2.cloned.1.call-done) | copy-start | bytes 5701636
  94.0 26.1 %copy-start.6 = (bf16[232,928]{1,0:T(8,128)(2,1)S(1)}, bf16[232,928]{1,0:T(8,128)(2,1)}, u32[]{:S(2)}) copy-start(bf16[232,928]{1,0:T(8,128)(2,1)} %moment.3) | copy-start | bytes 1291780
  98.0 16.3 %all-to-all-start.2 = ((f32[4,2,64,256]{3,2,1,0:T(8,128)}), f32[4,2,64,256]{3,2,1,0:T(8,128)}, u32[]{:S(2)}, u32[]{:S(2)}) async-start(f32[4,2,64,256]{3,2,1,0:T(8,128)} %shard_map.130), calls=%async_computation.2 | async-start | bytes 1048576 | tf_op jit(solution)/shard_map/all_to_all | solution.py:251
  107.1 18.5 %collective-permute-start.3 = (f32[64,512]{1,0:T(8,128)}, f32[64,512]{1,0:T(8,128)}, u32[]{:S(2)}, u32[]{:S(2)}) collective-permute-start(f32[64,512]{1,0:T(8,128)} %get-tuple-element.38), channel_id=1, source_target_pairs={{0,256},{256,0},{1,257},{257,1},{2,258},{258,2},{3,259},{259,3},{4... | collective-permute-start | bytes 393224 | tf_op jit(solution)/shard_map/ppermute | solution.py:253
  115.5 10.1 %collective-permute-start.4 = (f32[64,256]{1,0:T(8,128)S(1)}, f32[64,256]{1,0:T(8,128)S(1)}, u32[]{:S(2)}, u32[]{:S(2)}) collective-permute-start(f32[64,256]{1,0:T(8,128)S(1)} %get-tuple-element.41), channel_id=1, source_target_pairs={{0,256},{256,0},{1,257},{257,1},{2,258},{258,2},{3,259},{259,3},{4... | collective-permute-start | bytes 196616 | tf_op jit(solution)/shard_map/ppermute | solution.py:255
  120.1 1.1 copy-start.2
Sparse Core Ops, SparseCore 0:
  23.8 53.5 all-gather.1

commit v5 on v3

--- a/solution.py
+++ b/solution.py
@@ -233,12 +233,11 @@
     query_all, inputs = lax.optimization_barrier((query_all, inputs))
     query_theirs = token_half(1 - core, query_all, query_weight)
     query_theirs = lax.ppermute(query_theirs, "core", SWAP)
-    inputs_theirs = lax.ppermute(inputs, "core", SWAP)
     query_pair = token_half(core, query_all, query_weight, query_theirs, place=x_yh)
-    query_pair, inputs_theirs = lax.optimization_barrier((query_pair, inputs_theirs))
     query_parts = lax.all_to_all(query_pair, "x", 0, 0, tiled=True)
     output_theirs = token_half(1 - core, output_all, output_weight, fetch=True)
     output_theirs = lax.ppermute(output_theirs, "core", SWAP)
+    inputs_theirs = lax.ppermute(inputs, "core", SWAP)
     output_pair = token_half(
         core, output_all, output_weight, output_theirs, fetch=True, place=x_yh
     )

time: 133 us -> 133 us (level)
  no operation moved by 1% of the time
where the time goes in v5:
time: 133 us; the launch traced here: 132 us
  blocking collectives  50.7 us (38%)
  starting transfers between devices  40.1 us (30%)
  between operations  14.2 us (11%)
  Pallas kernels  13.9 us (10%)
  waiting for transfers between devices  7.8 us (6%)
  local copies, waits for them, and re-layouts  4.55 us (3%)
    all_gather x1, blocking collectives, on_device(): query_all = lax.all_gather(grads[:, :width], 'z', axis=0, tiled=True)  35.9 us
    all_gather x1, blocking collectives, on_device(): grads = lax.all_gather(grads, 'yl', axis=0, tiled=True)  14.8 us
    pallas_call x9, Pallas kernels, call(): pl.pallas_call(kernel, grid_spec=pltpu.PrefetchScalarGridSpec(num_scalar_...  13.9 us
    all_to_all x1, starting transfers between devices, on_device(): inputs = lax.all_to_all(inputs, ('yh', 'x'), 0, 0, tiled=True)  10.2 us
    ppermute x1, starting transfers between devices, on_device(): query_far = lax.ppermute(query_far, 'yh', SWAP)  7.42 us
    all_to_all x1, starting transfers between devices, on_device(): output_parts = lax.all_to_all(output_pair, 'x', 0, 0, tiled=True)  6.41 us
    ppermute x1, waiting for transfers between devices, on_device(): output_far = lax.ppermute(output_far, 'yh', SWAP)  5.92 us
    ppermute x1, starting transfers between devices, on_device(): output_far = lax.ppermute(output_far, 'yh', SWAP)  4.83 us
  transfers between devices with their start and end apart: 9, of which 3 were waited for; matrix products, arithmetic and copies ran while one was open for 1% of the time, Pallas kernels for 10%

profile of v5, /device:TPU:4, one launch (start us, length us, event | category | flops | bytes accessed | tf_op | source)
XLA Modules:
  0.0 132.2 jit_solution(13682565949412251168)
XLA Ops:
  7.2 0.9 concatenate.6
  8.2 14.8 %all_gather.9 = bf16[128,1440]{1,0:T(8,128)(2,1)S(1)} all-gather(bf16[32,1440]{1,0:T(8,128)(2,1)S(1)} %concatenate.6), channel_id=1, replica_groups=mesh['yh'=2,'x'=4,'core'=2,'z'=8,'yl'=4] {'yl'}, dimensions={0}, use_global_device_ids=true | all-gather | bytes 460800 | tf_op jit(solution)/shard_map/all_gather | solution.py:224
  23.8 0.9 pad_maximum_fusion
  24.7 0.9 broadcast_in_dim.14
  25.7 10.2 %all-to-all-start = ((bf16[8,64,744]{2,1,0:T(8,128)(2,1)}), bf16[8,64,744]{2,1,0:T(8,128)(2,1)S(1)}, u32[]{:S(2)}, u32[]{:S(2)}) async-start(bf16[8,64,744]{2,1,0:T(8,128)(2,1)} %broadcast_in_dim.14), calls=%async_computation | async-start | bytes 1572864 | tf_op jit(solution)/shard_map/all_to_all | solution.py:231
  35.9 35.9 %all_gather.10 = bf16[1024,464]{1,0:T(8,128)(2,1)S(1)} all-gather(bf16[128,464]{1,0:T(8,128)(2,1)S(1)} %slice.8), channel_id=1, replica_groups=mesh['yh'=2,'x'=4,'core'=2,'z'=8,'yl'=4] {'z'}, dimensions={0}, use_global_device_ids=true | all-gather | bytes 1069056 | tf_op jit(solution)/shard_map/all_gather | solution.py:232
  72.3 1.9 %collective-permute-start = (f32[512,512]{1,0:T(8,128)S(1)}, f32[512,512]{1,0:T(8,128)S(1)}, u32[]{:S(2)}, u32[]{:S(2)}) collective-permute-start(f32[512,512]{1,0:T(8,128)S(1)} %shard_map.127), channel_id=1, source_target_pairs={{0,32},{32,0},{1,33},{33,1},{2,34},{34,2},{3,35},{35,3},{4,36},{36... | collective-permute-start | bytes 3145736 | tf_op jit(solution)/shard_map/ppermute | solution.py:235
  74.2 2.4 %collective-permute-start.2 = (bf16[8,64,744]{2,1,0:T(8,128)(2,1)S(1)}, bf16[8,64,744]{2,1,0:T(8,128)(2,1)S(1)}, u32[]{:S(2)}, u32[]{:S(2)}) collective-permute-start(bf16[8,64,744]{2,1,0:T(8,128)(2,1)S(1)} %all-to-all-done.inputs), channel_id=1, source_target_pairs={{0,32},{32,0},{1,33},{33,1},{2,34},{34,2},{3,35},{35,3},{4,36},{36... | collective-permute-start | bytes 2285576 | tf_op jit(solution)/shard_map/ppermute | solution.py:240
  76.9 1.0 copy-done.3
  77.9 1.5 %shard_map.128 = f32[4,2,64,512]{3,2,1,0:T(8,128)} custom-call(s32[1]{0:T(128)} %bitcast.1.pick, bf16[8,2,64,464]{3,2,1,0:T(8,128)(2,1)S(1)} %bitcast.10, bf16[464,464]{1,0:T(8,128)(2,1)S(1)} %copy-done.3, f32[512,512]{1,0:T(8,128)S(1)} %collective-permute-done.rest_0_), custom_call_target="tpu_custom_call" | custom-call | flops 243269632 | bytes 2429440 | tf_op jit(solution)/shard_map/pallas_call | solution.py:43
  79.4 4.8 %all-to-all-start.1 = ((f32[4,2,64,512]{3,2,1,0:T(8,128)}), f32[4,2,64,512]{3,2,1,0:T(8,128)}, u32[]{:S(2)}, u32[]{:S(2)}) async-start(f32[4,2,64,512]{3,2,1,0:T(8,128)} %shard_map.128), calls=%async_computation.1 | async-start | bytes 2097152 | tf_op jit(solution)/shard_map/all_to_all | solution.py:237
  84.2 1.9 %shard_map.129 = f32[512,256]{1,0:T(8,128)S(1)} custom-call(s32[1]{0:T(128)} %bitcast.3.pick, bf16[8,2,64,928]{3,2,1,0:T(8,128)(2,1)} %bitcast.5, bf16[232,928]{1,0:T(8,128)(2,1)S(1)} %copy-done.1), custom_call_target="tpu_custom_call" | custom-call | flops 243269632 | bytes 2331136 | tf_op jit(solution)/shard_map/pallas_call | solution.py:43
  86.1 2.1 %collective-permute-start.1 = (f32[512,256]{1,0:T(8,128)S(1)}, f32[512,256]{1,0:T(8,128)S(1)}, u32[]{:S(2)}, u32[]{:S(2)}) collective-permute-start(f32[512,256]{1,0:T(8,128)S(1)} %shard_map.129), channel_id=1, source_target_pairs={{0,32},{32,0},{1,33},{33,1},{2,34},{34,2},{3,35},{35,3},{4,36},{36... | collective-permute-start | bytes 1572872 | tf_op jit(solution)/shard_map/ppermute | solution.py:239
  88.2 2.1 %shard_map.131 = (bf16[464,464]{1,0:T(8,128)(2,1)}, bf16[464,464]{1,0:T(8,128)(2,1)}) custom-call(s32[1]{0:T(128)} %bitcast.1.pick, bf16[8,64,744]{2,1,0:T(8,128)(2,1)S(1)} %all-to-all-done.inputs, bf16[8,64,744]{2,1,0:T(8,128)(2,1)S(1)} %collective-permute-done.2.inputs_theirs, bf16[8,2,64,464]{3,2,1,0:T(8,128)(2,1)S(1)} %bitcast.11, ...), custom_call_target="tpu_custom_call" | custom-call | flops 440926208 | bytes 3854848 | tf_op jit(solution)/shard_map/pallas_call | solution.py:43
  90.3 2.1 %shard_map.132 = (bf16[232,928]{1,0:T(8,128)(2,1)}, bf16[232,928]{1,0:T(8,128)(2,1)}) custom-call(s32[1]{0:T(128)} %bitcast.1.pick, bf16[8,64,744]{2,1,0:T(8,128)(2,1)S(1)} %all-to-all-done.inputs, bf16[8,64,744]{2,1,0:T(8,128)(2,1)S(1)} %collective-permute-done.2.inputs_theirs, bf16[8,2,64,928]{3,2,1,0:T(8,128)(2,1)S(1)} %bitcast.7, ...), custom_call_target="tpu_custom_call" | custom-call | flops 440926208 | bytes 5755392 | tf_op jit(solution)/shard_map/pallas_call | solution.py:43
  92.4 2.7 %shard_map.130 = f32[4,2,64,256]{3,2,1,0:T(8,128)} custom-call(s32[1]{0:T(128)} %bitcast.1.pick, bf16[8,2,64,928]{3,2,1,0:T(8,128)(2,1)} %bitcast.6, bf16[232,928]{1,0:T(8,128)(2,1)S(1)} %copy-done.1, f32[512,256]{1,0:T(8,128)S(1)} %collective-permute-done.1.rest_0_), custom_call_target="tpu_custom_call" | custom-call | flops 243269632 | bytes 2855424 | tf_op jit(solution)/shard_map/pallas_call | solution.py:43
  95.1 1.6 %all-to-all-done.1.parts = f32[4,2,64,512]{3,2,1,0:T(8,128)} async-done(((f32[4,2,64,512]{3,2,1,0:T(8,128)}), f32[4,2,64,512]{3,2,1,0:T(8,128)}, u32[]{:S(2)}, u32[]{:S(2)}) %all-to-all-start.1) | async-done | bytes 1048608 | tf_op jit(solution)/shard_map/all_to_all | solution.py:237
  96.7 6.4 %all-to-all-start.2 = ((f32[4,2,64,256]{3,2,1,0:T(8,128)}), f32[4,2,64,256]{3,2,1,0:T(8,128)S(1)}, u32[]{:S(2)}, u32[]{:S(2)}) async-start(f32[4,2,64,256]{3,2,1,0:T(8,128)} %shard_map.130), calls=%async_computation.2 | async-start | bytes 1048576 | tf_op jit(solution)/shard_map/all_to_all | solution.py:253
  103.1 1.4 %shard_map.133 = (f32[64,512]{1,0:T(8,128)S(1)}, f32[64,512]{1,0:T(8,128)S(1)}) custom-call(s32[1]{0:T(128)} %bitcast.pick, f32[4,2,64,512]{3,2,1,0:T(8,128)} %all-to-all-done.1.parts), custom_call_target="tpu_custom_call" | custom-call | bytes 1048576 | tf_op jit(solution)/shard_map/pallas_call | solution.py:43
  104.6 7.4 %collective-permute-start.3 = (f32[64,512]{1,0:T(8,128)S(1)}, f32[64,512]{1,0:T(8,128)S(1)}, u32[]{:S(2)}, u32[]{:S(2)}) collective-permute-start(f32[64,512]{1,0:T(8,128)S(1)} %get-tuple-element.34), channel_id=1, source_target_pairs={{0,256},{256,0},{1,257},{257,1},{2,258},{258,2},{3,259},{259,3},{4... | collective-permute-start | bytes 393224 | tf_op jit(solution)/shard_map/ppermute | solution.py:255
  112.0 0.8 copy-done.6
  112.8 1.2 shard_map.134
  114.0 4.8 %collective-permute-start.4 = (f32[64,256]{1,0:T(8,128)S(1)}, f32[64,256]{1,0:T(8,128)S(1)}, u32[]{:S(2)}, u32[]{:S(2)}) collective-permute-start(f32[64,256]{1,0:T(8,128)S(1)} %get-tuple-element.37), channel_id=1, source_target_pairs={{0,256},{256,0},{1,257},{257,1},{2,258},{258,2},{3,259},{259,3},{4... | collective-permute-start | bytes 196616 | tf_op jit(solution)/shard_map/ppermute | solution.py:257
  118.8 5.9 %collective-permute-done.4.refs_3_ = f32[64,256]{1,0:T(8,128)S(1)} collective-permute-done((f32[64,256]{1,0:T(8,128)S(1)}, f32[64,256]{1,0:T(8,128)S(1)}, u32[]{:S(2)}, u32[]{:S(2)}) %collective-permute-start.4) | collective-permute-done | bytes 65568 | tf_op jit(solution)/shard_map/ppermute | solution.py:257
  (28 shorter events, 2.2 us)
Async XLA Ops:
  7.2 77.0 %all-gather.2.cloned.1.call-start = ((), (), s32[]{:S(2)}) async-start(), calls=%async_computation.3 | async-start | bytes 2359296 | tf_op jit(solution)/shard_map/all_gather | solution.py:228
  23.7 48.1 %copy-start.2 = (bf16[464,464]{1,0:T(8,128)(2,1)S(1)}, bf16[464,464]{1,0:T(8,128)(2,1)}, u32[]{:S(2)}) copy-start(bf16[464,464]{1,0:T(8,128)(2,1)} %weight.5) | copy-start | bytes 1291780
  25.7 46.2 %all-to-all-start = ((bf16[8,64,744]{2,1,0:T(8,128)(2,1)}), bf16[8,64,744]{2,1,0:T(8,128)(2,1)S(1)}, u32[]{:S(2)}, u32[]{:S(2)}) async-start(bf16[8,64,744]{2,1,0:T(8,128)(2,1)} %broadcast_in_dim.14), calls=%async_computation | async-start | bytes 1572864 | tf_op jit(solution)/shard_map/all_to_all | solution.py:231
  72.3 4.6 %collective-permute-start = (f32[512,512]{1,0:T(8,128)S(1)}, f32[512,512]{1,0:T(8,128)S(1)}, u32[]{:S(2)}, u32[]{:S(2)}) collective-permute-start(f32[512,512]{1,0:T(8,128)S(1)} %shard_map.127), channel_id=1, source_target_pairs={{0,32},{32,0},{1,33},{33,1},{2,34},{34,2},{3,35},{35,3},{4,36},{36... | collective-permute-start | bytes 3145736 | tf_op jit(solution)/shard_map/ppermute | solution.py:235
  74.2 13.9 %collective-permute-start.2 = (bf16[8,64,744]{2,1,0:T(8,128)(2,1)S(1)}, bf16[8,64,744]{2,1,0:T(8,128)(2,1)S(1)}, u32[]{:S(2)}, u32[]{:S(2)}) collective-permute-start(bf16[8,64,744]{2,1,0:T(8,128)(2,1)S(1)} %all-to-all-done.inputs), channel_id=1, source_target_pairs={{0,32},{32,0},{1,33},{33,1},{2,34},{34,2},{3,35},{35,3},{4,36},{36... | collective-permute-start | bytes 2285576 | tf_op jit(solution)/shard_map/ppermute | solution.py:240
  76.9 1.0 copy-start.3
  77.9 6.3 %copy-start.1 = (bf16[232,928]{1,0:T(8,128)(2,1)S(1)}, bf16[232,928]{1,0:T(8,128)(2,1)}, u32[]{:S(2)}) copy-start(bf16[232,928]{1,0:T(8,128)(2,1)} %weight.7) | copy-start | bytes 1291780
  79.4 17.3 %all-to-all-start.1 = ((f32[4,2,64,512]{3,2,1,0:T(8,128)}), f32[4,2,64,512]{3,2,1,0:T(8,128)}, u32[]{:S(2)}, u32[]{:S(2)}) async-start(f32[4,2,64,512]{3,2,1,0:T(8,128)} %shard_map.128), calls=%async_computation.1 | async-start | bytes 2097152 | tf_op jit(solution)/shard_map/all_to_all | solution.py:237
  84.2 4.0 %copy-start.4 = (bf16[464,464]{1,0:T(8,128)(2,1)S(1)}, bf16[464,464]{1,0:T(8,128)(2,1)}, u32[]{:S(2)}) copy-start(bf16[464,464]{1,0:T(8,128)(2,1)} %moment.2) | copy-start | bytes 1291780
  86.1 4.2 %copy-start = (bf16[1024,928]{1,0:T(8,128)(2,1)S(1)}, bf16[1024,928]{1,0:T(8,128)(2,1)}, u32[]{:S(2)}) copy-start(bf16[1024,928]{1,0:T(8,128)(2,1)} %all-gather.2.cloned.1.call-done) | copy-start | bytes 5701636
  86.1 4.2 %copy-start.5 = (bf16[232,928]{1,0:T(8,128)(2,1)S(1)}, bf16[232,928]{1,0:T(8,128)(2,1)}, u32[]{:S(2)}) copy-start(bf16[232,928]{1,0:T(8,128)(2,1)} %moment.3) | copy-start | bytes 1291780
  86.1 6.3 %collective-permute-start.1 = (f32[512,256]{1,0:T(8,128)S(1)}, f32[512,256]{1,0:T(8,128)S(1)}, u32[]{:S(2)}, u32[]{:S(2)}) collective-permute-start(f32[512,256]{1,0:T(8,128)S(1)} %shard_map.129), channel_id=1, source_target_pairs={{0,32},{32,0},{1,33},{33,1},{2,34},{34,2},{3,35},{35,3},{4,36},{36... | collective-permute-start | bytes 1572872 | tf_op jit(solution)/shard_map/ppermute | solution.py:239
  96.7 15.2 %all-to-all-start.2 = ((f32[4,2,64,256]{3,2,1,0:T(8,128)}), f32[4,2,64,256]{3,2,1,0:T(8,128)S(1)}, u32[]{:S(2)}, u32[]{:S(2)}) async-start(f32[4,2,64,256]{3,2,1,0:T(8,128)} %shard_map.130), calls=%async_computation.2 | async-start | bytes 1048576 | tf_op jit(solution)/shard_map/all_to_all | solution.py:253
  104.6 14.3 %collective-permute-start.3 = (f32[64,512]{1,0:T(8,128)S(1)}, f32[64,512]{1,0:T(8,128)S(1)}, u32[]{:S(2)}, u32[]{:S(2)}) collective-permute-start(f32[64,512]{1,0:T(8,128)S(1)} %get-tuple-element.34), channel_id=1, source_target_pairs={{0,256},{256,0},{1,257},{257,1},{2,258},{258,2},{3,259},{259,3},{4... | collective-permute-start | bytes 393224 | tf_op jit(solution)/shard_map/ppermute | solution.py:255
  112.0 0.8 copy-start.6
  114.0 10.8 %collective-permute-start.4 = (f32[64,256]{1,0:T(8,128)S(1)}, f32[64,256]{1,0:T(8,128)S(1)}, u32[]{:S(2)}, u32[]{:S(2)}) collective-permute-start(f32[64,256]{1,0:T(8,128)S(1)} %get-tuple-element.37), channel_id=1, source_target_pairs={{0,256},{256,0},{1,257},{257,1},{2,258},{258,2},{3,259},{259,3},{4... | collective-permute-start | bytes 196616 | tf_op jit(solution)/shard_map/ppermute | solution.py:257
Sparse Core Ops, SparseCore 0:
  23.8 53.5 all-gather.1
